TPU v7x, 256 devices: a whole 4x4x8 slice. The times are simulated.
256 devices in a mesh: stretch: 32 (over z_lo, x, core), seq: 8 (over z_hi, y).
Axes of the slice: x: 4, y: 4, z: 8 (z_hi: 2, z_lo: 4; z = z_hi * 4 + z_lo), core: 2. Of those that a mesh axis runs over, the one named last changes fastest.
Arguments:
- queries: bfloat16 [12288, 24, 128], P(('stretch', 'seq')), may hold values from -48 to 48
- keys_values: bfloat16 [12288, 8, 256], P(('stretch', 'seq')), may hold values from -12 to 12
- out_weight: bfloat16 [3072, 6144], P('seq'), may hold values from -0.109375 to 0.109375
- latents: bfloat16 [12288, 6144], P(('stretch', 'seq')), may hold values from -6 to 6
- gate_table: float32 [64, 6144], replicated, may hold values from 0.5 to 1.5
- noise_level: int32 [32], replicated, may hold values from 0 to 63
- stretch_mask: int32 [32, 32], replicated, may hold values from 0 to 1, as said below
Outputs:
- next_latents: bfloat16 [12288, 6144], P(('stretch', 'seq'))
Inputs may be any that keep to these rules, and one draw needn't show every extreme that they name: stretch_mask[c, c] is 1 and stretch_mask[c, j] is 0 for j > c.
All inputs are finite; a program needn't handle non-finite values.
Results may differ from a plain program's by a relative error of at most 0.0095.
Values may be sent and summed in bfloat16 or wider, within the bound.
A program may use at most 64 MiB of HBM per device.

v0:
```python
import math

import jax
import jax.numpy as jnp
from jax import lax
from jax.sharding import PartitionSpec as P

NEG_START = -1e30


def shifted(value, axis, steps):
    count = lax.axis_size(axis)
    pairs = [(source, (source + steps) % count) for source in range(count)]
    return lax.ppermute(value, axis, pairs)


def attend_block(att_carry, query_rows, kv_block, score_scale):
    run_max, run_sum, accumulated = att_carry
    head_dim = query_rows.shape[-1]
    kv_heads = kv_block.shape[1]
    grouped = query_rows.reshape(query_rows.shape[0], kv_heads, -1, head_dim)
    key_part = kv_block[:, :, :head_dim]
    values = kv_block[:, :, head_dim:]
    scores = (
        jnp.einsum("qkgd,pkd->kgqp", grouped, key_part, preferred_element_type=jnp.float32)
        * score_scale
    )
    new_max = jnp.maximum(run_max, jnp.max(scores, axis=-1))
    factor = jnp.exp(run_max - new_max)
    weights = jnp.exp(scores - new_max[..., None])
    run_sum = run_sum * factor + jnp.sum(weights, axis=-1)
    update = jnp.einsum(
        "kgqp,pkd->kgqd", weights.astype(jnp.bfloat16), values, preferred_element_type=jnp.float32
    )
    accumulated = accumulated * factor[..., None] + update
    return (new_max, run_sum, accumulated)


def on_device(queries, keys_values, out_weight, latents, gate_table, noise_level, stretch_mask):
    stretch_here = lax.axis_index("stretch")
    stretch_count = lax.axis_size("stretch")
    local_q, local_kv = (
        lax.all_to_all(queries, "seq", split_axis=1, concat_axis=0, tiled=True),
        lax.all_to_all(keys_values, "seq", split_axis=1, concat_axis=0, tiled=True),
    )
    row_count, q_heads, head_dim = local_q.shape
    kv_heads = local_kv.shape[1]
    per_group = q_heads // kv_heads
    score_scale = 1.0 / math.sqrt(head_dim)
    visible = lax.dynamic_index_in_dim(stretch_mask, stretch_here, 0, keepdims=False)
    begin = (
        jnp.full((kv_heads, per_group, row_count), NEG_START, jnp.float32),
        jnp.zeros((kv_heads, per_group, row_count), jnp.float32),
        jnp.zeros((kv_heads, per_group, row_count, head_dim), jnp.float32),
    )
    att_carry = attend_block(begin, local_q, local_kv, score_scale)

    def maybe_attend(current, kv_block, source):
        safe_source = jnp.clip(source, 0, stretch_count - 1)
        flag = lax.dynamic_index_in_dim(visible, safe_source, 0, keepdims=False)
        is_seen = (source >= 0) & (source != stretch_here) & (flag == 1)
        return lax.cond(
            is_seen,
            lambda status: attend_block(status, local_q, kv_block, score_scale),
            lambda status: status,
            current,
        )

    kv_piece = lax.all_gather(local_kv[None], "stretch", axis=0, tiled=True)

    def visit(index, status):
        kv_block = lax.dynamic_index_in_dim(kv_piece, index, 0, keepdims=False)
        return maybe_attend(status, kv_block, index)

    att_carry = lax.fori_loop(0, kv_piece.shape[0], visit, att_carry)
    run_max, run_sum, accumulated = att_carry
    attended = accumulated / run_sum[..., None]
    attended = (
        jnp.transpose(attended, (2, 0, 1, 3))
        .reshape(row_count, q_heads * head_dim)
        .astype(jnp.bfloat16)
    )
    branch = lax.psum_scatter(
        jnp.dot(attended, out_weight, preferred_element_type=jnp.float32).astype(jnp.bfloat16),
        "seq",
        scatter_dimension=0,
        tiled=True,
    ).astype(jnp.float32)
    level_here = lax.dynamic_index_in_dim(noise_level, stretch_here, 0, keepdims=False)
    one_hot = (jnp.arange(gate_table.shape[0], dtype=jnp.int32) == level_here).astype(jnp.float32)
    gate_row = jnp.dot(one_hot, gate_table, precision=lax.Precision.HIGHEST)
    updated = (latents.astype(jnp.float32) + gate_row[None, :] * branch).astype(jnp.bfloat16)
    return shifted(updated, "stretch", 1)


def solution(mesh):
    in_specs = (
        P(("stretch", "seq"), None, None),
        P(("stretch", "seq"), None, None),
        P("seq", None),
        P(("stretch", "seq"), None),
        P(),
        P(),
        P(),
    )
    out_specs = P(("stretch", "seq"), None)
    return jax.shard_map(
        on_device, mesh=mesh, in_specs=in_specs, out_specs=out_specs, check_vma=False
    )
```

profile of v0, /device:TPU:8, one launch (start us, length us, event | category | flops | bytes accessed | tf_op | source)
XLA Modules:
  0.0 356.8 jit_solution(16492195197592275631)
XLA Ops:
  6.5 0.0 copy-start
  6.5 0.0 all-gather.2.cloned.1.call-start
  6.5 1.1 copy.21
  7.6 20.6 %all_to_all.33 = bf16[48,8,256]{2,0,1:T(8,128)(2,1)} all-to-all(bf16[48,8,256]{2,0,1:T(8,128)(2,1)S(1)} %copy.21), channel_id=1, replica_groups=mesh['stretch'=32,'seq'=8] {'seq'}, dimensions={1} | all-to-all | bytes 393216 | tf_op jit(solution)/shard_map/all_to_all | solution.py:44
  28.2 0.0 copy-start.1
  28.2 0.0 all-gather.2.cloned.1.call-update
  28.2 1.8 copy.22
  30.0 5.0 %all-to-all-start.1 = ((bf16[48,24,128]{2,0,1:T(8,128)(2,1)}), bf16[48,24,128]{2,0,1:T(8,128)(2,1)S(1)}, u32[]{:S(2)}, u32[]{:S(2)}) async-start(bf16[48,24,128]{2,0,1:T(8,128)(2,1)} %copy.22), calls=%async_computation.1 | async-start | bytes 589824 | tf_op jit(solution)/shard_map/all_to_all | solution.py:43
  35.0 0.0 reduce-scatter.2.cloned.1.call-start
  35.0 0.7 dynamic-slice_bitcast_fusion.1
  35.7 8.8 %all-to-all-done.1 = bf16[48,24,128]{2,0,1:T(8,128)(2,1)S(1)} async-done(((bf16[48,24,128]{2,0,1:T(8,128)(2,1)}), bf16[48,24,128]{2,0,1:T(8,128)(2,1)S(1)}, u32[]{:S(2)}, u32[]{:S(2)}) %all-to-all-start.1) | async-done | bytes 294944 | tf_op jit(solution)/shard_map/all_to_all | solution.py:43
  44.5 0.0 copy-done.1
  44.5 0.4 bitcast_reduce_fusion.1
  45.0 0.3 fusion.13
  45.3 0.5 fusion.14
  45.9 47.3 %all-gather.2.cloned.1.call-done = bf16[32,384,1,256]{3,1,2,0:T(8,128)(2,1)} async-done(((bf16[1,384,1,256]{3,1,2,0:T(8,128)(2,1)}), bf16[32,384,1,256]{3,1,2,0:T(8,128)(2,1)}) %all-gather.2.cloned.1.call-update) | async-done | bytes 6291472 | tf_op jit(solution)/shard_map/all_gather | solution.py:69
  93.1 41.4 %while.17 = (s32[]{:T(128)}, f32[1,3,384]{2,1,0:T(4,128)S(1)}, f32[1,3,384]{2,1,0:T(4,128)S(1)}, f32[1,3,384,128]{3,2,1,0:T(8,128)S(1)}, s32[]{:T(128)}, /*index...) while((s32[]{:T(128)}, f32[1,3,384]{2,1,0:T(4,128)S(1)}, ...), condition=%wide.region_7.8_spmd, body=%wide.region_2.7_spmd.sunk | while | flops 230329744 | bytes 7449933 | solution.py:75
  93.1 0.6 dynamic_slice.33
  94.4 0.6 dynamic_slice.33
  95.7 0.6 dynamic_slice.33
  97.0 0.6 dynamic_slice.33
  98.3 0.6 dynamic_slice.33
  99.6 0.6 dynamic_slice.33
  100.9 0.6 dynamic_slice.33
  102.2 0.6 dynamic_slice.33
  103.5 0.6 dynamic_slice.33
  104.8 0.6 dynamic_slice.33
  106.1 0.6 dynamic_slice.33
  107.4 0.6 dynamic_slice.33
  108.6 0.6 dynamic_slice.33
  109.9 0.6 dynamic_slice.33
  111.2 0.6 dynamic_slice.33
  112.5 0.6 dynamic_slice.33
  113.8 0.6 dynamic_slice.33
  115.1 0.6 dynamic_slice.33
  116.4 0.6 dynamic_slice.33
  117.7 0.6 dynamic_slice.33
  119.0 0.6 dynamic_slice.33
  120.3 0.6 dynamic_slice.33
  121.6 0.6 dynamic_slice.33
  122.9 0.6 dynamic_slice.33
  124.2 0.6 dynamic_slice.33
  125.5 0.6 dynamic_slice.33
  126.8 0.6 dynamic_slice.33
  128.1 0.6 dynamic_slice.33
  129.4 0.6 dynamic_slice.33
  130.7 0.6 dynamic_slice.33
  132.0 0.6 dynamic_slice.33
  133.2 0.6 dynamic_slice.33
  134.5 0.2 copy.25
  134.8 0.1 divide_convert_fusion
  134.8 7.1 %convolution_convert_fusion = bf16[384,6144]{1,0:T(8,128)(2,1)} fusion(bf16[384,384]{0,1:T(8,128)(2,1)S(1)} %bitcast.112, bf16[384,6144]{1,0:T(8,128)(2,1)} %param.13), kind=kOutput, calls=%fused_computation.19 | convolution fusion | flops 1814298624 | bytes 9732096 | tf_op jit(solution)/shard_map/dot_general | solution.py:84
  141.9 0.0 copy-start.3
  141.9 0.0 reduce-scatter.2.cloned.1.call-update
  142.0 0.6 copy-done.3
  142.6 0.6 dynamic_slice.28
  143.2 0.0 copy-done
  143.2 1.3 fusion.20
  144.4 190.1 %reduce-scatter.2.cloned.1.call-done = bf16[48,6144]{1,0:T(8,128)(2,1)} async-done(((bf16[384,6144]{1,0:T(8,128)(2,1)}), bf16[48,6144]{1,0:T(8,128)(2,1)}) %reduce-scatter.2.cloned.1.call-update) | async-done | bytes 589840 | tf_op jit(solution)/shard_map/reduce_scatter | solution.py:83
  334.6 0.0 copy-done.2
  334.6 1.2 add_convert_fusion
  335.8 0.1 collective-permute-start
  335.9 13.2 %collective-permute-done = bf16[48,6144]{1,0:T(8,128)(2,1)S(1)} collective-permute-done((bf16[48,6144]{1,0:T(8,128)(2,1)S(1)}, bf16[48,6144]{1,0:T(8,128)(2,1)S(1)}, u32[]{:S(2)}, u32[]{:S(2)}) %collective-permute-start) | collective-permute-done | bytes 589856 | tf_op jit(solution)/shard_map/ppermute | solution.py:14
  349.1 0.8 copy.47
  (36 shorter events, 0.5 us)
Async XLA Ops:
  6.5 136.6 %copy-start = (f32[64,6144]{1,0:T(8,128)S(1)}, f32[64,6144]{1,0:T(8,128)}, u32[]{:S(2)}) copy-start(f32[64,6144]{1,0:T(8,128)} %param.15) | copy-start | bytes 4718596
  6.5 86.6 %all-gather.2.cloned.1.call-start = ((), (), s32[]{:S(2)}) async-start(), calls=%async_computation.3 | async-start | bytes 6488064 | tf_op jit(solution)/shard_map/all_gather | solution.py:69
  28.2 16.3 %copy-start.1 = (bf16[48,8,256]{2,0,1:T(8,128)(2,1)S(1)}, bf16[48,8,256]{2,0,1:T(8,128)(2,1)}, u32[]{:S(2)}) copy-start(bf16[48,8,256]{2,0,1:T(8,128)(2,1)} %all_to_all.33) | copy-start | bytes 589828
  30.0 14.5 %all-to-all-start.1 = ((bf16[48,24,128]{2,0,1:T(8,128)(2,1)}), bf16[48,24,128]{2,0,1:T(8,128)(2,1)S(1)}, u32[]{:S(2)}, u32[]{:S(2)}) async-start(bf16[48,24,128]{2,0,1:T(8,128)(2,1)} %copy.22), calls=%async_computation.1 | async-start | bytes 589824 | tf_op jit(solution)/shard_map/all_to_all | solution.py:43
  35.0 299.6 %reduce-scatter.2.cloned.1.call-start = ((), (), s32[]{:S(2)}) async-start(), calls=%async_computation.4 | async-start | bytes 5308416 | tf_op jit(solution)/shard_map/reduce_scatter | solution.py:83
  141.9 0.7 copy-start.3
  142.6 192.0 %copy-start.2 = (bf16[48,6144]{1,0:T(8,128)(2,1)S(1)}, bf16[48,6144]{1,0:T(8,128)(2,1)}, u32[]{:S(2)}) copy-start(bf16[48,6144]{1,0:T(8,128)(2,1)} %param.14) | copy-start | bytes 1769476
  335.8 13.3 %collective-permute-start = (bf16[48,6144]{1,0:T(8,128)(2,1)S(1)}, bf16[48,6144]{1,0:T(8,128)(2,1)S(1)}, u32[]{:S(2)}, u32[]{:S(2)}) collective-permute-start(bf16[48,6144]{1,0:T(8,128)(2,1)S(1)} %add_convert_fusion), channel_id=1, source_target_pairs={{0,8},{8,16},{16,24},{24,32},{32,40},{40,48},{48,56},{56,64},{64,7... | collective-permute-start | bytes 1769480 | tf_op jit(solution)/shard_map/ppermute | solution.py:14
Sparse Core Ops, SparseCore 0:
  28.4 64.7 all-gather.1
  142.1 192.4 reduce-scatter.1
where the time goes:
time: 360 us; the launch traced here: 357 us
  waiting for transfers between devices  259 us (72%)
  local copies, waits for them, and re-layouts  24.6 us (7%)
  loops' own time  22.6 us (6%)
  blocking collectives  20.6 us (6%)
  between operations  13.5 us (4%)
  matrix products  9.33 us (3%)
  starting transfers between devices  5.11 us (1%)
    reduce_scatter x1, waiting for transfers between devices, on_device(): lax.psum_scatter(jnp.dot(attended, out_weight, preferred_element_type=jnp...  190 us
    all_gather x1, waiting for transfers between devices, on_device(): kv_piece = lax.all_gather(local_kv[None], 'stretch', axis=0, tiled=True)  47.3 us
    another operation x1, loops' own time, on_device(): att_carry = lax.fori_loop(0, kv_piece.shape[0], visit, att_carry)  22.2 us
    all_to_all x1, blocking collectives, on_device(): lax.all_to_all(keys_values, 'seq', split_axis=1, concat_axis=0, tiled=True)  20.6 us
    dynamic_slice x32, local copies, waits for them, and re-layouts, maybe_attend(): flag = lax.dynamic_index_in_dim(visible, safe_source, 0, keepdims=False)  18.8 us
    ppermute x1, waiting for transfers between devices, shifted(): return lax.ppermute(value, axis, pairs)  13.2 us
    all_to_all x1, waiting for transfers between devices, on_device(): lax.all_to_all(queries, 'seq', split_axis=1, concat_axis=0, tiled=True)  8.79 us
  transfers between devices with their start and end apart: 4, of which 4 were waited for; matrix products, arithmetic and copies ran while one was open for 2% of the time, Pallas kernels for 0%

commit v1 on v0

v1 whole, which is shorter than its diff:
```python
import functools
import math

import jax
import jax.numpy as jnp
from jax import lax
from jax.experimental import pallas as pl
from jax.experimental.pallas import tpu as pltpu
from jax.sharding import PartitionSpec as P

MESH = pl.DeviceIdType.MESH
BIG = 1e30
MIB = 2**20

ROWS = 48
CT = 384
HD = 128
GROUP = 3
SEQ = 8
QROWS = CT * GROUP
D = 6144
EXP_SCALE = math.log2(math.e) / math.sqrt(HD)

NC = 4
CW = D // (2 * NC)


def position():
    c = lax.axis_index("stretch")
    s = lax.axis_index("seq")
    return c, s


def push(src, dst, send, recv, target):
    return pltpu.make_async_remote_copy(
        src_ref=src, dst_ref=dst, send_sem=send, recv_sem=recv, device_id=target, device_id_type=MESH
    )


def greet(targets):
    barrier = pltpu.get_barrier_semaphore()
    for target in targets:
        pl.semaphore_signal(barrier, inc=1, device_id=target, device_id_type=MESH)
    pl.semaphore_wait(barrier, len(targets))


def attention_kernel(
    q_ref, kv_ref, hide_ref, att_ref,
    kvr, qr, qt, slots, acc, run_max, run_sum,
    kv_send, kv_recv, q_send, q_recv, z_send, x_send, sib_send, slot_recv,
):
    c, s = position()
    z, x, k = c // 8, (c // 2) % 4, c % 2

    def dev(zz, xx, kk):
        return ((zz * 4 + xx) * 2 + kk, s)

    greet(
        [(c, (s + d) % SEQ) for d in range(1, SEQ)]
        + [dev((z + d) % 4, x, k) for d in (1, 2, 3)]
        + [dev(z, (x + d) % 4, k) for d in (1, 2, 3)]
        + [dev(z, x, 1 - k)]
    )

    def kv_copy(d):
        other = (s + d) % SEQ
        return push(kv_ref.at[other], kvr.at[s], kv_send.at[d], kv_recv.at[s], (c, other))

    def q_copy(d):
        other = (s + d) % SEQ
        return push(q_ref.at[other], qr.at[s], q_send.at[d], q_recv.at[s], (c, other))

    def landed(ref, recv, index):
        push(ref.at[index], ref.at[index], kv_send.at[0], recv.at[index], (c, (s + 1) % SEQ)).wait_recv()

    for d in (4, 3, 5, 2, 6, 1, 7):
        kv_copy(d).start()
    for d in (4, 3, 5, 2, 6, 1, 7):
        q_copy(d).start()
    kvr[s] = kv_ref[s]
    qr[s] = q_ref[s]
    run_max[...] = jnp.full_like(run_max, -BIG)
    run_sum[...] = jnp.zeros_like(run_sum)
    acc[...] = jnp.zeros_like(acc)
    for d in range(1, SEQ):
        landed(kvr, kv_recv, (s + d) % SEQ)
    block = kvr[...].reshape(CT, 2 * HD)
    slots[c, 0:CT, :] = block[:, :HD]
    value_t = jnp.transpose(block[:, HD:].astype(jnp.float32)).astype(jnp.bfloat16)
    for t in range(3):
        slots[c, CT + t * HD : CT + (t + 1) * HD, :] = value_t[:, t * HD : (t + 1) * HD]

    def slot_push(j, send, target):
        return push(slots.at[j], slots.at[j], send, slot_recv.at[j], target)

    def z_copy(d):
        return slot_push(c, z_send.at[d - 1], dev((z + d) % 4, x, k))

    def x_copy(t, d):
        return slot_push(dev(z - t, x, k)[0], x_send.at[t, d - 1], dev(z, (x + d) % 4, k))

    def pair_of(n):
        t, i = n // 4, n % 4
        step = i + i // 2 - 2 * (i // 3)
        return (z - t) * 4 + (x + step) % 4

    def sib_copy(n):
        return slot_push(2 * pair_of(n) + k, sib_send.at[n], dev(z, x, 1 - k))

    def wait_slot(j):
        slot_push(j, z_send.at[0], dev(z, x, 1 - k)).wait_recv()

    def spread(t):
        for d in (1, 3, 2):
            x_copy(t, d).start()
        sib_copy(4 * t).start()

    def forward(n):
        wait_slot(2 * pair_of(n) + k)
        sib_copy(n).start()

    sib_copy(0).start()
    for d in (1, 2, 3):
        @pl.when(z + d < 4)
        def _(d=d):
            z_copy(d).start()
    for d in (1, 3, 2):
        x_copy(0, d).start()

    for d in range(1, SEQ):
        landed(qr, q_recv, (s + d) % SEQ)
    qt[...] = jnp.transpose(qr[...].reshape(QROWS, HD).astype(jnp.float32)).astype(jnp.bfloat16)

    own_pair = z * 4 + x

    def attend(pair):
        ja = 2 * pair
        hide_a, hide_b = hide_ref[ja], hide_ref[ja + 1]

        def values(j):
            return jnp.concatenate(
                [slots[j, CT + t * HD : CT + (t + 1) * HD, :] for t in range(3)], axis=1
            )

        va, vb = values(ja), values(ja + 1)
        ka, kb = slots[ja, 0:CT, :], slots[ja + 1, 0:CT, :]
        for r in range(GROUP):
            cols = slice(r * CT, (r + 1) * CT)
            q_cols = qt[:, cols]
            sa = jnp.dot(ka, q_cols, preferred_element_type=jnp.float32)
            sb = jnp.dot(kb, q_cols, preferred_element_type=jnp.float32)
            top = jnp.maximum(
                jnp.max(sa, axis=0, keepdims=True) - hide_a, jnp.max(sb, axis=0, keepdims=True) - hide_b
            )
            old = run_max[:, cols]
            new = jnp.maximum(old, top)
            factor = jnp.exp2((old - new) * EXP_SCALE)
            pa = jnp.exp2((sa - (new + hide_a)) * EXP_SCALE)
            pb = jnp.exp2((sb - (new + hide_b)) * EXP_SCALE)
            run_max[:, cols] = new
            run_sum[:, cols] = (
                run_sum[:, cols] * factor
                + jnp.sum(pa, axis=0, keepdims=True)
                + jnp.sum(pb, axis=0, keepdims=True)
            )
            acc[:, cols] = (
                acc[:, cols] * factor
                + jnp.dot(va, pa.astype(jnp.bfloat16), preferred_element_type=jnp.float32)
                + jnp.dot(vb, pb.astype(jnp.bfloat16), preferred_element_type=jnp.float32)
            )

    def step(n, carry):
        t, i = n // 4, n % 4
        pair = pair_of(n)
        wait_slot(2 * pair + 1 - k)

        @pl.when(pair <= own_pair)
        def _():
            attend(pair)

        @pl.when((i == 0) & (t < z))
        def _():
            wait_slot(dev(z - t - 1, x, k)[0])
            spread(t + 1)

        @pl.when(n == 0)
        def _():
            forward(1)

        @pl.when((i < 2) | ((i == 3) & (t < z)))
        def _():
            forward(n + 2)

        return carry

    total = 4 * (z + 1)
    lax.fori_loop(0, total, step, 0)

    out = jnp.transpose(acc[...] * (1.0 / run_sum[...])).astype(jnp.bfloat16)
    att_ref[...] = out.reshape(SEQ, GROUP, ROWS, HD)

    for d in range(1, SEQ):
        kv_copy(d).wait_send()
        q_copy(d).wait_send()
    for d in (1, 2, 3):
        @pl.when(z + d < 4)
        def _(d=d):
            z_copy(d).wait_send()

    def drain_x(t, carry):
        for d in (1, 2, 3):
            x_copy(t, d).wait_send()
        return carry

    def drain_sib(n, carry):
        sib_copy(n).wait_send()
        return carry

    lax.fori_loop(0, z + 1, drain_x, 0)
    lax.fori_loop(0, total, drain_sib, 0)


def attention(q_t, kv_t, hide):
    flops = 4 * QROWS * HD * CT * 24
    return pl.pallas_call(
        attention_kernel,
        out_shape=jax.ShapeDtypeStruct((SEQ, GROUP, ROWS, HD), jnp.bfloat16),
        in_specs=[
            pl.BlockSpec(memory_space=pltpu.VMEM),
            pl.BlockSpec(memory_space=pltpu.VMEM),
            pl.BlockSpec(memory_space=pltpu.SMEM),
        ],
        out_specs=pl.BlockSpec(memory_space=pltpu.VMEM),
        scratch_shapes=[
            pltpu.VMEM((SEQ, ROWS, 2 * HD), jnp.bfloat16),
            pltpu.VMEM((SEQ, GROUP, ROWS, HD), jnp.bfloat16),
            pltpu.VMEM((HD, QROWS), jnp.bfloat16),
            pltpu.VMEM((32, 2 * CT, HD), jnp.bfloat16),
            pltpu.VMEM((HD, QROWS), jnp.float32),
            pltpu.VMEM((1, QROWS), jnp.float32),
            pltpu.VMEM((1, QROWS), jnp.float32),
            pltpu.SemaphoreType.DMA((SEQ,)),
            pltpu.SemaphoreType.DMA((SEQ,)),
            pltpu.SemaphoreType.DMA((SEQ,)),
            pltpu.SemaphoreType.DMA((SEQ,)),
            pltpu.SemaphoreType.DMA((3,)),
            pltpu.SemaphoreType.DMA((4, 3)),
            pltpu.SemaphoreType.DMA((16,)),
            pltpu.SemaphoreType.DMA((32,)),
        ],
        compiler_params=pltpu.CompilerParams(
            collective_id=0, has_side_effects=True, vmem_limit_bytes=32 * MIB
        ),
        cost_estimate=pl.CostEstimate(flops=flops, bytes_accessed=60 * MIB, transcendentals=QROWS * CT * 24),
        name="attention",
    )(q_t, kv_t, hide)


def project_kernel(
    att_ref, own_ref, other_ref, lat_ref, gate_ref, out_ref,
    att_in, weights, part, sends, recvs, done,
    w_sem, att_sem, ring_send, ring_recv, out_send, out_recv,
):
    c, s = position()
    zh, y = s // 4, s % 4
    partner = (c, (s + 4) % SEQ)
    up, down = (c, zh * 4 + (y + 1) % 4), (c, zh * 4 + (y + 3) % 4)
    after, before = ((c + 1) % 32, s), ((c + 31) % 32, s)

    def load(q):
        return [
            pltpu.make_async_copy(own_ref.at[:, pl.ds(q * CW, CW)], weights.at[0, q], w_sem.at[q, 0]),
            pltpu.make_async_copy(other_ref.at[2 * q], weights.at[1, q, :, 0:CT], w_sem.at[q, 1]),
            pltpu.make_async_copy(other_ref.at[2 * q + 1], weights.at[1, q, :, CT : 2 * CT], w_sem.at[q, 2]),
        ]

    for j in range(NC):
        for copy in load(j) + load(NC + j):
            copy.start()
    greet([partner, up, down, after, before])
    swap = push(
        att_ref.at[pl.ds(4 * (1 - zh), 4)], att_in, att_sem.at[0], att_sem.at[1], partner
    )
    swap.start()

    def ring(step, dirn, j):
        target = up if dirn == 0 else down
        return push(
            sends.at[step, dirn, j], recvs.at[step, dirn, j],
            ring_send.at[step, dirn, j], ring_recv.at[step, dirn, j], target,
        )

    def block_at(step, dirn):
        return (y + 3 - step) % 4 if dirn == 0 else (y + 1 + step) % 4

    def rows_of(att):
        heads = [att[:, h].reshape(4 * ROWS, HD) for h in range(GROUP)]
        return jnp.concatenate(heads, axis=1)

    own_rows = rows_of(att_ref[pl.ds(4 * zh, 4)])
    swap.wait()
    other_rows = rows_of(att_in[...])

    def first(j, carry):
        for dirn in range(2):
            q = dirn * NC + j
            for copy in load(q):
                copy.wait()
            product = jnp.dot(own_rows, weights[0, q], preferred_element_type=jnp.float32)
            product = product + jnp.dot(other_rows, weights[1, q], preferred_element_type=jnp.float32)
            part[q] = product.reshape(4, ROWS, CW)
            sends[0, dirn, j] = part[q, block_at(0, dirn)].astype(jnp.bfloat16)
            ring(0, dirn, j).start()
        return carry

    lax.fori_loop(0, NC, first, 0)

    for step in (1, 2):
        def middle(j, carry, step=step):
            for dirn in range(2):
                q = dirn * NC + j
                ring(step - 1, dirn, j).wait_recv()
                sends[step, dirn, j] = (
                    recvs[step - 1, dirn, j].astype(jnp.float32) + part[q, block_at(step, dirn)]
                ).astype(jnp.bfloat16)
                ring(step, dirn, j).start()
            return carry

        lax.fori_loop(0, NC, middle, 0)

    def final(q):
        cols = pl.ds(pl.multiple_of(q * CW, CW), CW)
        return push(done.at[:, cols], out_ref.at[:, cols], out_send.at[q], out_recv.at[q], after)

    def last(j, carry):
        for dirn in range(2):
            q = dirn * NC + j
            cols = pl.ds(pl.multiple_of(q * CW, CW), CW)
            ring(2, dirn, j).wait_recv()
            branch = recvs[2, dirn, j].astype(jnp.float32) + part[q, y]
            done[:, cols] = (
                lat_ref[:, cols].astype(jnp.float32) + gate_ref[:, cols] * branch
            ).astype(jnp.bfloat16)
            final(q).start()
        return carry

    lax.fori_loop(0, NC, last, 0)

    def drain(j, carry):
        for dirn in range(2):
            for step in range(3):
                ring(step, dirn, j).wait_send()
            final(dirn * NC + j).wait()
        return carry

    lax.fori_loop(0, NC, drain, 0)


def project(att, own, other, latents, gate_row):
    vmem = pl.BlockSpec(memory_space=pltpu.VMEM)
    anywhere = pl.BlockSpec(memory_space=pl.ANY)
    return pl.pallas_call(
        project_kernel,
        out_shape=jax.ShapeDtypeStruct((ROWS, D), jnp.bfloat16),
        in_specs=[vmem, anywhere, anywhere, vmem, vmem],
        out_specs=vmem,
        scratch_shapes=[
            pltpu.VMEM((4, GROUP, ROWS, HD), jnp.bfloat16),
            pltpu.VMEM((2, 2 * NC, CT, CW), jnp.bfloat16),
            pltpu.VMEM((2 * NC, 4, ROWS, CW), jnp.float32),
            pltpu.VMEM((3, 2, NC, ROWS, CW), jnp.bfloat16),
            pltpu.VMEM((3, 2, NC, ROWS, CW), jnp.bfloat16),
            pltpu.VMEM((ROWS, D), jnp.bfloat16),
            pltpu.SemaphoreType.DMA((2 * NC, 3)),
            pltpu.SemaphoreType.DMA((2,)),
            pltpu.SemaphoreType.DMA((3, 2, NC)),
            pltpu.SemaphoreType.DMA((3, 2, NC)),
            pltpu.SemaphoreType.DMA((2 * NC,)),
            pltpu.SemaphoreType.DMA((2 * NC,)),
        ],
        compiler_params=pltpu.CompilerParams(
            collective_id=1, has_side_effects=True, vmem_limit_bytes=40 * MIB
        ),
        cost_estimate=pl.CostEstimate(flops=4 * CT * CT * D, bytes_accessed=12 * MIB, transcendentals=0),
        name="project",
    )(att, own, other, latents, gate_row)


def partner_weights(out_weight, c):
    half, chip = c % 2, c // 2
    piece = lax.dynamic_slice(out_weight, (half * (CT // 2), chip * CT), (CT // 2, CT))
    piece = lax.ppermute(piece, "seq", [(i, (i + 4) % SEQ) for i in range(SEQ)])
    return lax.all_gather(piece, "stretch", axis=0, tiled=True).reshape(16, CT, CT)


def on_device(queries, keys_values, out_weight, latents, gate_table, noise_level, stretch_mask):
    c = lax.axis_index("stretch")
    other = partner_weights(out_weight, c)
    q_t = jnp.transpose(queries.reshape(ROWS, SEQ, GROUP, HD), (1, 2, 0, 3))
    kv_t = jnp.transpose(keys_values, (1, 0, 2))
    visible = lax.dynamic_index_in_dim(stretch_mask, c, 0, keepdims=False)
    hide = jnp.where(visible == 1, 0.0, BIG).astype(jnp.float32)
    att = attention(q_t, kv_t, hide)
    level = lax.dynamic_index_in_dim(noise_level, c, 0, keepdims=False)
    gate_row = lax.dynamic_slice(gate_table, (level, 0), (1, D))
    return project(att, out_weight, other, latents, gate_row)


def solution(mesh):
    rows = P(("stretch", "seq"), None)
    heads = P(("stretch", "seq"), None, None)
    return jax.shard_map(
        on_device,
        mesh=mesh,
        in_specs=(heads, heads, P("seq", None), rows, P(), P(), P()),
        out_specs=rows,
        check_vma=False,
    )
```

time: 360 us -> 166 us (0.46)
  waiting for transfers between devices: 259 us -> 48.8 us
  Pallas kernels: 0 us -> 82.6 us
  loops' own time: 22.6 us -> 0 us
  blocking collectives: 20.6 us -> 0 us
  local copies, waits for them, and re-layouts: 24.6 us -> 10.5 us
  matrix products: 9.33 us -> 0 us
    reduce_scatter x1 -> x0, waiting for transfers between devices: 190 us -> none  [on_device(): lax.psum_scatter(jnp.dot(attended, out_weight, preferred_element_type=jnp...]
    pallas_call x0 -> x2, Pallas kernels: none -> 82.6 us  [the longest x1 42.6 us: attention(): pl.pallas_call(attention_kernel, out_shape=jax.ShapeDtypeStruct((SEQ, GRO...]
    another operation x33 -> x0, loops' own time: 22.6 us -> none  [the longest x1 22.2 us: on_device(): att_carry = lax.fori_loop(0, kv_piece.shape[0], visit, att_carry)]
    all_to_all x1 -> x0, blocking collectives: 20.6 us -> none  [on_device(): lax.all_to_all(keys_values, 'seq', split_axis=1, concat_axis=0, tiled=True)]
    dynamic_slice x33 -> x3, local copies, waits for them, and re-layouts: 19.4 us -> 2.39 us  [the longest x1 1.32 us: on_device(): level = lax.dynamic_index_in_dim(noise_level, c, 0, keepdims=False)]
    dot_general x4 -> x0, matrix products: 9.33 us -> none  [the longest x1 7.11 us: on_device(): jnp.dot(attended, out_weight, preferred_element_type=jnp.float32)]
    ppermute x1, waiting for transfers between devices: 13.2 us -> 3.95 us  [partner_weights(): piece = lax.ppermute(piece, 'seq', [(i, (i + 4) % SEQ) for i in range(SEQ)])]
    all_to_all x1 -> x0, waiting for transfers between devices: 8.79 us -> none  [on_device(): lax.all_to_all(queries, 'seq', split_axis=1, concat_axis=0, tiled=True)]
  transfers between devices with their start and end apart: 4 -> 2, of which waited for: 4 -> 2; matrix products, arithmetic and copies ran while one was open for 2% -> 2% of each run, Pallas kernels for 0% -> 26%
where the time goes in v1:
time: 166 us; the launch traced here: 165 us
  Pallas kernels  82.6 us (50%)
  waiting for transfers between devices  48.8 us (29%)
  between operations  15.5 us (9%)
  local copies, waits for them, and re-layouts  10.5 us (6%)
  starting transfers between devices  7.28 us (4%)
    all_gather x1, waiting for transfers between devices, partner_weights(): lax.all_gather(piece, 'stretch', axis=0, tiled=True).reshape(16, CT, CT)  44.8 us
    pallas_call x1, Pallas kernels, attention(): pl.pallas_call(attention_kernel, out_shape=jax.ShapeDtypeStruct((SEQ, GRO...  42.6 us
    pallas_call x1, Pallas kernels, project(): pl.pallas_call(project_kernel, out_shape=jax.ShapeDtypeStruct((ROWS, D),...  40 us
    unnamed x13, local copies, waits for them, and re-layouts  8.13 us
    ppermute x1, starting transfers between devices, partner_weights(): piece = lax.ppermute(piece, 'seq', [(i, (i + 4) % SEQ) for i in range(SEQ)])  7.28 us
    ppermute x1, waiting for transfers between devices, partner_weights(): piece = lax.ppermute(piece, 'seq', [(i, (i + 4) % SEQ) for i in range(SEQ)])  3.95 us
  transfers between devices with their start and end apart: 2, of which 2 were waited for; matrix products, arithmetic and copies ran while one was open for 2% of the time, Pallas kernels for 26%

profile of v1, /device:TPU:8, one launch (start us, length us, event | category | flops | bytes accessed | tf_op | source)
XLA Modules:
  0.0 165.4 jit_solution(12057825409259374545)
XLA Ops:
  6.5 0.0 copy-start
  6.5 0.0 all-gather.2.cloned.1.call-start
  6.5 1.0 dynamic_slice.15
  7.6 7.3 %collective-permute-start = (bf16[192,384]{1,0:T(8,128)(2,1)S(1)}, bf16[192,384]{1,0:T(8,128)(2,1)S(1)}, u32[]{:S(2)}, u32[]{:S(2)}) collective-permute-start(bf16[192,384]{1,0:T(8,128)(2,1)S(1)} %dynamic_slice.15), channel_id=1, source_target_pairs={{0,4},{1,5},{2,6},{3,7},{4,0},{5,1},{6,2},{7,3},{8,12},{9,13},{10,... | collective-permute-start | bytes 442376 | tf_op jit(solution)/shard_map/ppermute | solution.py:392
  14.9 4.0 %collective-permute-done = bf16[192,384]{1,0:T(8,128)(2,1)S(1)} collective-permute-done((bf16[192,384]{1,0:T(8,128)(2,1)S(1)}, bf16[192,384]{1,0:T(8,128)(2,1)S(1)}, u32[]{:S(2)}, u32[]{:S(2)}) %collective-permute-start) | collective-permute-done | bytes 147488 | tf_op jit(solution)/shard_map/ppermute | solution.py:392
  18.8 0.0 copy-start.4
  18.8 0.7 copy-done.4
  19.5 0.0 all-gather.2.cloned.1.call-update
  19.5 1.3 dynamic_slice.16
  22.2 1.0 copy.11
  23.2 1.0 copy.8
  24.9 0.7 fusion.hide_ref
  25.6 0.0 copy-start.3
  25.6 42.6 %attention.1.att_ref = bf16[8,3,48,128]{3,2,1,0:T(8,128)(2,1)S(1)} custom-call(bf16[8,3,48,128]{3,2,1,0:T(8,128)(2,1)S(1)} %bitcast.10, bf16[8,48,256]{2,1,0:T(8,128)(2,1)S(1)} %bitcast.11, f32[32]{0:T(128)S(1)} %fusion.hide_ref), custom_call_target="tpu_custom_call" | custom-call | flops 5435817984 | bytes 62914560 | tf_op jit(solution)/shard_map/attention/pallas_call | solution.py:225
  68.2 0.0 copy-done
  68.3 44.8 %all-gather.2.cloned.1.call-done = bf16[6144,384]{1,0:T(8,128)(2,1)} async-done(((bf16[192,384]{1,0:T(8,128)(2,1)}), bf16[6144,384]{1,0:T(8,128)(2,1)}) %all-gather.2.cloned.1.call-update) | async-done | bytes 4718608 | tf_op jit(solution)/shard_map/all_gather | solution.py:393
  113.1 0.0 copy-done.3
  113.1 0.0 copy-start.1
  113.1 2.3 %copy-done.1 = bf16[384,6144]{1,0:T(8,128)(2,1)S(1)} copy-done((bf16[384,6144]{1,0:T(8,128)(2,1)S(1)}, bf16[384,6144]{1,0:T(8,128)(2,1)}, u32[]{:S(2)}) %copy-start.1) | copy-done | bytes 4718616
  115.4 0.0 copy-start.2
  115.4 2.3 %copy-done.2 = bf16[6144,384]{1,0:T(8,128)(2,1)S(1)} copy-done((bf16[6144,384]{1,0:T(8,128)(2,1)S(1)}, bf16[6144,384]{1,0:T(8,128)(2,1)}, u32[]{:S(2)}) %copy-start.2) | copy-done | bytes 4718616
  117.8 40.0 %project.1 = bf16[48,6144]{1,0:T(8,128)(2,1)S(1)} custom-call(bf16[8,3,48,128]{3,2,1,0:T(8,128)(2,1)S(1)} %attention.1.att_ref, bf16[384,6144]{1,0:T(8,128)(2,1)S(1)} %copy-done.1, bf16[16,384,384]{2,1,0:T(8,128)(2,1)S(1)} %bitcast.12, bf16[48,6144]{1,0:T(8,128)(2,1)S(1)} %copy-done.3, f32[1,6144]{1,0:T(1,128)S(1)} %constant_dynamic-slice_fusion.gate_ref), custom_call_target="tpu_custom_call" | custom-call | flops 3623878656 | bytes 12582912 | tf_op jit(solution)/shard_map/project/pallas_call | solution.py:362
  157.8 0.8 copy.13
  (1 shorter events, 0.0 us)
Async XLA Ops:
  6.5 61.7 %copy-start = (f32[64,6144]{1,0:T(8,128)S(1)}, f32[64,6144]{1,0:T(8,128)}, u32[]{:S(2)}) copy-start(f32[64,6144]{1,0:T(8,128)} %param.11) | copy-start | bytes 4718596
  6.5 106.5 %all-gather.2.cloned.1.call-start = ((), (), s32[]{:S(2)}) async-start(), calls=%async_computation | async-start | bytes 4866048 | tf_op jit(solution)/shard_map/all_gather | solution.py:393
  7.6 11.2 %collective-permute-start = (bf16[192,384]{1,0:T(8,128)(2,1)S(1)}, bf16[192,384]{1,0:T(8,128)(2,1)S(1)}, u32[]{:S(2)}, u32[]{:S(2)}) collective-permute-start(bf16[192,384]{1,0:T(8,128)(2,1)S(1)} %dynamic_slice.15), channel_id=1, source_target_pairs={{0,4},{1,5},{2,6},{3,7},{4,0},{5,1},{6,2},{7,3},{8,12},{9,13},{10,... | collective-permute-start | bytes 442376 | tf_op jit(solution)/shard_map/ppermute | solution.py:392
  18.8 0.7 copy-start.4
  25.6 87.5 %copy-start.3 = (bf16[48,6144]{1,0:T(8,128)(2,1)S(1)}, bf16[48,6144]{1,0:T(8,128)(2,1)}, u32[]{:S(2)}) copy-start(bf16[48,6144]{1,0:T(8,128)(2,1)} %lat_ref.1) | copy-start | bytes 1769476
  113.1 2.3 %copy-start.1 = (bf16[384,6144]{1,0:T(8,128)(2,1)S(1)}, bf16[384,6144]{1,0:T(8,128)(2,1)}, u32[]{:S(2)}) copy-start(bf16[384,6144]{1,0:T(8,128)(2,1)} %own_ref.1) | copy-start | bytes 14155780
  115.4 2.3 %copy-start.2 = (bf16[6144,384]{1,0:T(8,128)(2,1)S(1)}, bf16[6144,384]{1,0:T(8,128)(2,1)}, u32[]{:S(2)}) copy-start(bf16[6144,384]{1,0:T(8,128)(2,1)} %all-gather.2.cloned.1.call-done) | copy-start | bytes 14155780
Sparse Core Ops, SparseCore 0:
  19.6 93.4 all-gather.1

commit v2 on v1

v2 whole, which is shorter than its diff:
```python
import math

import jax
import jax.numpy as jnp
from jax import lax
from jax.experimental import pallas as pl
from jax.experimental.pallas import tpu as pltpu
from jax.sharding import PartitionSpec as P

MESH = pl.DeviceIdType.MESH
BIG = 1e30
MIB = 2**20
F32, BF16 = jnp.float32, jnp.bfloat16

ROWS = 48
CT = 384
HD = 128
GROUP = 3
SEQ = 8
QROWS = CT * GROUP
D = 6144
EXP_SCALE = math.log2(math.e) / math.sqrt(HD)

NC = 4
CW = D // (2 * NC)
CHUNKS = 16
DOWN = 10
HALF = CT // 2


def kernel(
    q_ref, kv_ref, mask_ref, level_ref, own_hbm, lat_hbm, gate_hbm, out_ref,
    kvr, qr, qt, slots, acc, run_max, run_sum, att, att_in, rows_in,
    own_w, other_w, part, sends, recvs, lat, gate, done,
    kv_send, kv_recv, q_send, q_recv, z_send, x_send, relay_send, sib_send, slot_recv, half_recv,
    load_sem, w_send, w_sib_send, w_recv, swap_sem, ring_send, ring_recv, out_send, out_recv,
):
    c = lax.axis_index("stretch")
    s = lax.axis_index("seq")
    z, x, k = c // 8, (c // 2) % 4, c % 2
    zh, y = s // 4, s % 4

    def dev(zz, xx, kk):
        return ((zz * 4 + xx) * 2 + kk, s)

    def z_next(step):
        pos = (zh * 4 + z + step + 8) % 8
        return (((pos % 4) * 4 + x) * 2 + k, (pos // 4) * 4 + y)

    sibling = dev(z, x, 1 - k)
    above, below = z_next(1), z_next(-1)
    x_right, x_left = dev(z, (x + 1) % 4, k), dev(z, (x + 3) % 4, k)
    partner = (c, (s + 4) % SEQ)
    y_up, y_down = (c, zh * 4 + (y + 1) % 4), (c, zh * 4 + (y + 3) % 4)
    after, before = ((c + 1) % 32, s), ((c + 31) % 32, s)

    def push(src, dst, send, recv, target):
        return pltpu.make_async_remote_copy(
            src_ref=src, dst_ref=dst, send_sem=send, recv_sem=recv, device_id=target, device_id_type=MESH
        )

    def load_own(b):
        return pltpu.make_async_copy(own_hbm.at[:, pl.ds(b * CT, CT)], own_w.at[b], load_sem.at[b])

    load_lat = pltpu.make_async_copy(lat_hbm, lat, load_sem.at[CHUNKS])
    load_gate = pltpu.make_async_copy(gate_hbm, gate, load_sem.at[CHUNKS + 1])

    barrier = pltpu.get_barrier_semaphore()
    greeted = [(c, (s + d) % SEQ) for d in range(1, SEQ)] + [
        above, below, x_right, x_left, sibling, after, before,
    ]
    for target in greeted:
        pl.semaphore_signal(barrier, inc=1, device_id=target, device_id_type=MESH)
    pl.semaphore_wait(barrier, len(greeted))

    def kv_copy(d):
        other = (s + d) % SEQ
        return push(kv_ref.at[other], kvr.at[s], kv_send.at[d], kv_recv.at[s], (c, other))

    def q_copy(d):
        other = (s + d) % SEQ
        return push(q_ref.at[other], qr.at[s], q_send.at[d], q_recv.at[s], (c, other))

    def landed(ref, recv, index):
        push(ref.at[index], ref.at[index], kv_send.at[0], recv.at[index], partner).wait_recv()

    for d in (4, 3, 5, 2, 6, 1, 7):
        kv_copy(d).start()
    for d in (4, 3, 5, 2, 6, 1, 7):
        q_copy(d).start()
    for b in range(CHUNKS):
        load_own(b).start()
    load_lat.start()
    load_gate.start()
    kvr[s] = kv_ref[s]
    qr[s] = q_ref[s]
    run_max[...] = jnp.full_like(run_max, -BIG)
    run_sum[...] = jnp.zeros_like(run_sum)
    acc[...] = jnp.zeros_like(acc)
    for d in range(1, SEQ):
        landed(kvr, kv_recv, (s + d) % SEQ)
    block = kvr[...].reshape(CT, 2 * HD)
    slots[c, 0:CT, :] = block[:, :HD]
    value_t = jnp.transpose(block[:, HD:].astype(F32)).astype(BF16)
    for t in range(3):
        slots[c, CT + t * HD : CT + (t + 1) * HD, :] = value_t[:, t * HD : (t + 1) * HD]

    def slot_push(j, send, target):
        return push(slots.at[j], slots.at[j], send, slot_recv.at[j], target)

    def column_slot(t):
        return ((z - t) * 4 + x) * 2 + k

    def z_copy(t):
        return slot_push(column_slot(t), z_send.at[t], above)

    def x_copy(t, right):
        return slot_push(column_slot(t), x_send.at[t, right], x_right if right else x_left)

    def pair_of(n):
        t, i = n // 4, n % 4
        step = i + i // 2 - 2 * (i // 3)
        return (z - t) * 4 + (x + step) % 4

    def sib_copy(n):
        return slot_push(2 * pair_of(n) + k, sib_send.at[n], sibling)

    def half_of(t, pair, right):
        part_of = slots.at[2 * pair + k, pl.ds(CT * right, CT)]
        return push(
            part_of, part_of, relay_send.at[t, right], half_recv.at[t, right], x_right if right else x_left
        )

    def relay(t, right):
        return half_of(t, (z - t) * 4 + (x + 1 + 2 * right) % 4, right)

    def wait_slot(j):
        slot_push(j, z_send.at[0], sibling).wait_recv()

    def spread(t):
        @pl.when(z < 3)
        def _():
            z_copy(t).start()

        x_copy(t, 0).start()
        x_copy(t, 1).start()
        sib_copy(4 * t).start()

    def from_beside(t, right):
        n = 4 * t + 1 + right
        wait_slot(2 * pair_of(n) + k)
        relay(t, right).start()
        sib_copy(n).start()

    def from_across(t):
        n = 4 * t + 3
        for right in range(2):
            half_of(t, pair_of(n), right).wait_recv()
        sib_copy(n).start()

    def w_slice(ref, half, u):
        return ref.at[half * 8 + u // 2, pl.ds((u % 2) * HALF, HALF)]

    def w_push(u, own, target):
        source = w_slice(own_w if own else other_w, k, u)
        return push(source, w_slice(other_w, k, u), w_send.at[u], w_recv.at[k, u], target)

    def w_sib(u):
        piece = w_slice(other_w, k, u)
        return push(piece, piece, w_sib_send.at[u], w_recv.at[k, u], sibling)

    def w_relay(u, edge, target):
        w_push(u, False, target).wait_recv()

        @pl.when(z != edge)
        def _():
            w_push(u, False, target).start()

        w_sib(u).start()

    spread(0)
    for d in range(1, SEQ):
        landed(qr, q_recv, (s + d) % SEQ)
    qt[...] = jnp.transpose(qr[...].reshape(QROWS, HD).astype(F32)).astype(BF16)
    for b in range(CHUNKS):
        load_own(b).wait()

    @pl.when(z == 0)
    def _():
        def origin(u, carry):
            w_push(u, True, below).start()
            return carry

        lax.fori_loop(0, DOWN, origin, 0)

    own_pair = z * 4 + x

    def attend(pair):
        ja = 2 * pair
        hide_a = jnp.where(mask_ref[c, ja] == 1, 0.0, BIG).astype(F32)
        hide_b = jnp.where(mask_ref[c, ja + 1] == 1, 0.0, BIG).astype(F32)
        ones = jnp.ones((16, CT), BF16)

        def values(j):
            cut = [slots[j, CT + t * HD : CT + (t + 1) * HD, :] for t in range(3)]
            return jnp.concatenate([jnp.concatenate(cut, axis=1), ones], axis=0)

        va, vb = values(ja), values(ja + 1)
        ka, kb = slots[ja, 0:CT, :], slots[ja + 1, 0:CT, :]

        def score(r):
            q_cols = qt[:, r * CT : (r + 1) * CT]
            return (
                jnp.dot(ka, q_cols, preferred_element_type=F32),
                jnp.dot(kb, q_cols, preferred_element_type=F32),
            )

        ready = score(0)
        for r in range(GROUP):
            ahead = score(r + 1) if r + 1 < GROUP else None
            sa, sb = ready
            cols = slice(r * CT, (r + 1) * CT)
            top = jnp.maximum(
                jnp.max(sa, axis=0, keepdims=True) - hide_a, jnp.max(sb, axis=0, keepdims=True) - hide_b
            )
            old = run_max[:, cols]
            new = jnp.maximum(old, top)
            factor = jnp.exp2((old - new) * EXP_SCALE)
            pa = jnp.exp2((sa - (new + hide_a)) * EXP_SCALE)
            pb = jnp.exp2((sb - (new + hide_b)) * EXP_SCALE)
            run_max[:, cols] = new
            update = jnp.dot(va, pa.astype(BF16), preferred_element_type=F32) + jnp.dot(
                vb, pb.astype(BF16), preferred_element_type=F32
            )
            run_sum[:, cols] = run_sum[:, cols] * factor + update[HD : HD + 1]
            acc[:, cols] = acc[:, cols] * factor + update[:HD]
            ready = ahead

    first_relay = 8 - 2 * z

    def step(n, carry):
        t, i = n // 4, n % 4
        pair = pair_of(n)
        wait_slot(2 * pair + 1 - k)

        @pl.when(pair <= own_pair)
        def _():
            attend(pair)

        @pl.when((i == 0) & (t < z))
        def _():
            wait_slot(column_slot(t + 1))
            spread(t + 1)

        @pl.when(n == 0)
        def _():
            from_beside(0, 0)
            from_beside(0, 1)

        @pl.when(i == 1)
        def _():
            from_across(t)

        @pl.when((i == 3) & (t < z))
        def _():
            from_beside(t + 1, 0)
            from_beside(t + 1, 1)

        @pl.when((z == 3) & (n < CHUNKS - DOWN))
        def _():
            w_push(DOWN + n, True, above).start()

        @pl.when((n >= first_relay) & (n % 2 == 0) & (n < first_relay + 2 * DOWN))
        def _():
            w_relay((n - first_relay) // 2, 0, below)

        return carry

    total = 4 * (z + 1)
    lax.fori_loop(0, total, step, 0)

    out = jnp.transpose(acc[...] * (1.0 / run_sum[...])).astype(BF16)
    att[...] = out.reshape(SEQ, GROUP, ROWS, HD)
    swap = push(att.at[pl.ds(4 * (1 - zh), 4)], att_in, swap_sem.at[0], swap_sem.at[1], partner)
    swap.start()

    def late(u, carry):
        @pl.when(u >= (6 * z - 3) // 2)
        def _():
            w_relay(u, 0, below)

        @pl.when(u < CHUNKS - DOWN)
        def _():
            w_relay(DOWN + u, 3, above)

        return carry

    lax.fori_loop(0, DOWN, late, 0)

    def gather_rows(source, first, place):
        for h in range(GROUP):
            rows_in[place, :, h * HD : (h + 1) * HD] = source[pl.ds(first, 4), h].reshape(4 * ROWS, HD)

    gather_rows(att, 4 * zh, 0)
    swap.wait()
    gather_rows(att_in, 0, 1)

    def ring(hop, dirn, j):
        return push(
            sends.at[hop, dirn, j], recvs.at[hop, dirn, j],
            ring_send.at[hop, dirn, j], ring_recv.at[hop, dirn, j], y_down if dirn else y_up,
        )

    def block_at(hop, dirn):
        return (y + 1 + hop) % 4 if dirn else (y + 3 - hop) % 4

    def first(j, carry):
        for b in range(4):
            w_from = w_slice(other_w, 1 - k, 4 * j + b)
            push(w_from, w_from, w_sib_send.at[0], w_recv.at[1 - k, 4 * j + b], sibling).wait_recv()
        for dirn in range(2):
            q = dirn * NC + j
            for b in range(2):
                product = jnp.dot(rows_in[0], own_w[2 * q + b], preferred_element_type=F32)
                product += jnp.dot(rows_in[1], other_w[2 * q + b], preferred_element_type=F32)
                part[q, :, :, b * CT : (b + 1) * CT] = product.reshape(4, ROWS, CT)
            sends[0, dirn, j] = part[q, block_at(0, dirn)].astype(BF16)
            ring(0, dirn, j).start()
        return carry

    lax.fori_loop(0, NC, first, 0)

    for hop in (1, 2):
        def middle(j, carry, hop=hop):
            for dirn in range(2):
                q = dirn * NC + j
                ring(hop - 1, dirn, j).wait_recv()
                sends[hop, dirn, j] = (
                    recvs[hop - 1, dirn, j].astype(F32) + part[q, block_at(hop, dirn)]
                ).astype(BF16)
                ring(hop, dirn, j).start()
            return carry

        lax.fori_loop(0, NC, middle, 0)

    load_lat.wait()
    load_gate.wait()
    level = level_ref[c]

    def final(q):
        cols = pl.ds(pl.multiple_of(q * CW, CW), CW)
        return push(done.at[:, cols], out_ref.at[:, cols], out_send.at[q], out_recv.at[q], after)

    def last(j, carry):
        for dirn in range(2):
            q = dirn * NC + j
            cols = pl.ds(pl.multiple_of(q * CW, CW), CW)
            ring(2, dirn, j).wait_recv()
            branch = recvs[2, dirn, j].astype(F32) + part[q, y]
            gate_row = gate[pl.ds(level, 1), cols]
            done[:, cols] = (lat[:, cols].astype(F32) + gate_row * branch).astype(BF16)
            final(q).start()
        return carry

    lax.fori_loop(0, NC, last, 0)

    for d in range(1, SEQ):
        kv_copy(d).wait_send()
        q_copy(d).wait_send()

    def drain_plane(t, carry):
        @pl.when(z < 3)
        def _():
            z_copy(t).wait_send()

        for right in range(2):
            x_copy(t, right).wait_send()
            relay(t, right).wait_send()
        return carry

    def drain_sib(n, carry):
        sib_copy(n).wait_send()
        return carry

    def drain_w(u, carry):
        w_push(u, False, below).wait_send()
        w_sib(u).wait_send()
        return carry

    def drain_ring(j, carry):
        for dirn in range(2):
            for hop in range(3):
                ring(hop, dirn, j).wait_send()
            final(dirn * NC + j).wait()
        return carry

    lax.fori_loop(0, z + 1, drain_plane, 0)
    lax.fori_loop(0, total, drain_sib, 0)
    lax.fori_loop(0, CHUNKS, drain_w, 0)
    lax.fori_loop(0, NC, drain_ring, 0)


def fused(q_t, kv_t, mask, level, own, latents, gate_table):
    vmem = pl.BlockSpec(memory_space=pltpu.VMEM)
    smem = pl.BlockSpec(memory_space=pltpu.SMEM)
    anywhere = pl.BlockSpec(memory_space=pl.ANY)
    dma = pltpu.SemaphoreType.DMA
    return pl.pallas_call(
        kernel,
        out_shape=jax.ShapeDtypeStruct((ROWS, D), BF16),
        in_specs=[vmem, vmem, smem, smem, anywhere, anywhere, anywhere],
        out_specs=vmem,
        scratch_shapes=[
            pltpu.VMEM((SEQ, ROWS, 2 * HD), BF16),
            pltpu.VMEM((SEQ, GROUP, ROWS, HD), BF16),
            pltpu.VMEM((HD, QROWS), BF16),
            pltpu.VMEM((32, 2 * CT, HD), BF16),
            pltpu.VMEM((HD, QROWS), F32),
            pltpu.VMEM((1, QROWS), F32),
            pltpu.VMEM((1, QROWS), F32),
            pltpu.VMEM((SEQ, GROUP, ROWS, HD), BF16),
            pltpu.VMEM((4, GROUP, ROWS, HD), BF16),
            pltpu.VMEM((2, 4 * ROWS, CT), BF16),
            pltpu.VMEM((CHUNKS, CT, CT), BF16),
            pltpu.VMEM((CHUNKS, CT, CT), BF16),
            pltpu.VMEM((2 * NC, 4, ROWS, CW), F32),
            pltpu.VMEM((3, 2, NC, ROWS, CW), BF16),
            pltpu.VMEM((3, 2, NC, ROWS, CW), BF16),
            pltpu.VMEM((ROWS, D), BF16),
            pltpu.VMEM((64, D), F32),
            pltpu.VMEM((ROWS, D), BF16),
            dma((SEQ,)), dma((SEQ,)), dma((SEQ,)), dma((SEQ,)),
            dma((4,)), dma((4, 2)), dma((4, 2)), dma((16,)), dma((32,)), dma((4, 2)),
            dma((CHUNKS + 2,)), dma((CHUNKS,)), dma((CHUNKS,)), dma((2, CHUNKS)), dma((2,)),
            dma((3, 2, NC)), dma((3, 2, NC)), dma((2 * NC,)), dma((2 * NC,)),
        ],
        compiler_params=pltpu.CompilerParams(
            collective_id=0, has_side_effects=True, vmem_limit_bytes=48 * MIB
        ),
        cost_estimate=pl.CostEstimate(
            flops=4 * QROWS * HD * CT * 24, bytes_accessed=20 * MIB, transcendentals=QROWS * CT * 24
        ),
        name="stretch_attention",
    )(q_t, kv_t, mask, level, own, latents, gate_table)


def on_device(queries, keys_values, out_weight, latents, gate_table, noise_level, stretch_mask):
    q_t = jnp.transpose(queries.reshape(ROWS, SEQ, GROUP, HD), (1, 2, 0, 3))
    kv_t = jnp.transpose(keys_values, (1, 0, 2))
    return fused(q_t, kv_t, stretch_mask, noise_level, out_weight, latents, gate_table)


def solution(mesh):
    rows = P(("stretch", "seq"), None)
    heads = P(("stretch", "seq"), None, None)
    return jax.shard_map(
        on_device,
        mesh=mesh,
        in_specs=(heads, heads, P("seq", None), rows, P(), P(), P()),
        out_specs=rows,
        check_vma=False,
    )
```

time: 166 us -> 178 us (1.072)
  Pallas kernels: 82.6 us -> 169 us
  waiting for transfers between devices: 48.8 us -> 0 us
  between operations: 15.5 us -> 0.03 us
  starting transfers between devices: 7.28 us -> 0 us
  local copies, waits for them, and re-layouts: 10.5 us -> 6.62 us
    pallas_call x2 -> x1, Pallas kernels: 82.6 us -> 169 us  [fused(): pl.pallas_call(kernel, out_shape=jax.ShapeDtypeStruct((ROWS, D), BF16), i...]
    all_gather x1 -> x0, waiting for transfers between devices: 44.8 us -> none  [partner_weights(): lax.all_gather(piece, 'stretch', axis=0, tiled=True).reshape(16, CT, CT)]
    ppermute x1 -> x0, starting transfers between devices: 7.28 us -> none  [partner_weights(): piece = lax.ppermute(piece, 'seq', [(i, (i + 4) % SEQ) for i in range(SEQ)])]
    ppermute x1 -> x0, waiting for transfers between devices: 3.95 us -> none  [partner_weights(): piece = lax.ppermute(piece, 'seq', [(i, (i + 4) % SEQ) for i in range(SEQ)])]
    dynamic_slice x3 -> x0, local copies, waits for them, and re-layouts: 2.39 us -> none  [the longest x1 1.32 us: on_device(): level = lax.dynamic_index_in_dim(noise_level, c, 0, keepdims=False)]
    unnamed x13 -> x11, local copies, waits for them, and re-layouts: 8.13 us -> 6.62 us
  transfers between devices with their start and end apart: 2 -> 0, of which waited for: 2 -> 0; matrix products, arithmetic and copies ran while one was open for 2% -> 0% of each run, Pallas kernels for 26% -> 0%
where the time goes in v2:
time: 178 us; the launch traced here: 176 us
  Pallas kernels  169 us (95%)
  local copies, waits for them, and re-layouts  6.62 us (4%)
    pallas_call x1, Pallas kernels, fused(): pl.pallas_call(kernel, out_shape=jax.ShapeDtypeStruct((ROWS, D), BF16), i...  169 us
    unnamed x11, local copies, waits for them, and re-layouts  6.62 us

profile of v2, /device:TPU:8, one launch (start us, length us, event | category | flops | bytes accessed | tf_op | source)
XLA Modules:
  0.0 176.1 jit_solution(6502869190197677056)
XLA Ops:
  0.0 1.0 copy.11
  1.0 1.0 copy.8
  2.0 0.0 copy-start
  2.0 1.4 copy-done
  3.4 0.0 copy-start.1
  3.4 1.1 copy-done.1
  4.4 0.0 copy-start.2
  4.5 0.7 copy-done.2
  5.2 0.0 copy-start.3
  5.2 0.7 copy-done.3
  5.8 169.4 %stretch_attention.1 = bf16[48,6144]{1,0:T(8,128)(2,1)S(1)} custom-call(bf16[8,3,48,128]{3,2,1,0:T(8,128)(2,1)S(1)} %bitcast.6, bf16[8,48,256]{2,1,0:T(8,128)(2,1)S(1)} %bitcast.7, s32[32,32]{1,0:T(8,128)S(1)} %copy-done.2, s32[32]{0:T(128)S(1)} %copy-done.3, bf16[384,6144]{1,0:T(8,128)(2,1)} %own_hbm.1, bf16[48,6144]{1,0:T(8,128)(2,1)S(1)} %copy-done.1, ...), custom_call_target="tpu_custom_call" | custom-call | flops 5435817984 | bytes 20971520 | tf_op jit(solution)/shard_map/stretch_attention/pallas_call | solution.py:408
  175.3 0.8 copy.13
Async XLA Ops:
  2.0 1.4 copy-start
  3.4 1.1 copy-start.1
  4.4 0.7 copy-start.2
  5.2 0.7 copy-start.3

commit v3 on v2

--- a/solution.py
+++ b/solution.py
@@ -21,11 +21,8 @@
 D = 6144
 EXP_SCALE = math.log2(math.e) / math.sqrt(HD)
 
-NC = 4
-CW = D // (2 * NC)
-CHUNKS = 16
-DOWN = 10
-HALF = CT // 2
+NC = 8
+BLOCKS = 16
 
 
 def kernel(
@@ -33,7 +30,7 @@
     kvr, qr, qt, slots, acc, run_max, run_sum, att, att_in, rows_in,
     own_w, other_w, part, sends, recvs, lat, gate, done,
     kv_send, kv_recv, q_send, q_recv, z_send, x_send, relay_send, sib_send, slot_recv, half_recv,
-    load_sem, w_send, w_sib_send, w_recv, swap_sem, ring_send, ring_recv, out_send, out_recv,
+    load_sem, w_edge_send, w_send, w_sib_send, w_recv, swap_sem, ring_send, ring_recv, out_send, out_recv,
 ):
     c = lax.axis_index("stretch")
     s = lax.axis_index("seq")
@@ -48,8 +45,9 @@
         return (((pos % 4) * 4 + x) * 2 + k, (pos // 4) * 4 + y)
 
     sibling = dev(z, x, 1 - k)
-    above, below = z_next(1), z_next(-1)
-    x_right, x_left = dev(z, (x + 1) % 4, k), dev(z, (x + 3) % 4, k)
+    above = z_next(1)
+    outward = 2 * (z // 3) - 1
+    x_right, x_left, x_across = (dev(z, (x + d) % 4, k) for d in (1, 3, 2))
     partner = (c, (s + 4) % SEQ)
     y_up, y_down = (c, zh * 4 + (y + 1) % 4), (c, zh * 4 + (y + 3) % 4)
     after, before = ((c + 1) % 32, s), ((c + 31) % 32, s)
@@ -62,12 +60,12 @@
     def load_own(b):
         return pltpu.make_async_copy(own_hbm.at[:, pl.ds(b * CT, CT)], own_w.at[b], load_sem.at[b])
 
-    load_lat = pltpu.make_async_copy(lat_hbm, lat, load_sem.at[CHUNKS])
-    load_gate = pltpu.make_async_copy(gate_hbm, gate, load_sem.at[CHUNKS + 1])
+    load_lat = pltpu.make_async_copy(lat_hbm, lat, load_sem.at[BLOCKS])
+    load_gate = pltpu.make_async_copy(gate_hbm, gate, load_sem.at[BLOCKS + 1])
 
     barrier = pltpu.get_barrier_semaphore()
     greeted = [(c, (s + d) % SEQ) for d in range(1, SEQ)] + [
-        above, below, x_right, x_left, sibling, after, before,
+        z_next(1), z_next(-1), z_next(2), z_next(-2), x_right, x_left, x_across, sibling, after, before,
     ]
     for target in greeted:
         pl.semaphore_signal(barrier, inc=1, device_id=target, device_id_type=MESH)
@@ -88,7 +86,7 @@
         kv_copy(d).start()
     for d in (4, 3, 5, 2, 6, 1, 7):
         q_copy(d).start()
-    for b in range(CHUNKS):
+    for b in range(BLOCKS):
         load_own(b).start()
     load_lat.start()
     load_gate.start()
@@ -158,40 +156,49 @@
             half_of(t, pair_of(n), right).wait_recv()
         sib_copy(n).start()
 
-    def w_slice(ref, half, u):
-        return ref.at[half * 8 + u // 2, pl.ds((u % 2) * HALF, HALF)]
-
-    def w_push(u, own, target):
-        source = w_slice(own_w if own else other_w, k, u)
-        return push(source, w_slice(other_w, k, u), w_send.at[u], w_recv.at[k, u], target)
-
-    def w_sib(u):
-        piece = w_slice(other_w, k, u)
-        return push(piece, piece, w_sib_send.at[u], w_recv.at[k, u], sibling)
-
-    def w_relay(u, edge, target):
-        w_push(u, False, target).wait_recv()
-
-        @pl.when(z != edge)
-        def _():
-            w_push(u, False, target).start()
-
-        w_sib(u).start()
+    def block_of(place):
+        group = place // 4
+        step = group + group // 2 - 2 * (group // 3)
+        return 4 * ((x + step) % 4) + place % 4
+
+    def w_push(source, b, send, target):
+        return push(source.at[b], other_w.at[b], send, w_recv.at[b], target)
+
+    def w_edge(half, hop):
+        return w_push(own_w, 4 * x + 2 * k + half, w_edge_send.at[half, hop - 1], z_next(hop * outward))
+
+    def w_side(half, way):
+        target = (x_right, x_left, x_across, sibling)[way]
+        return w_push(other_w, 4 * x + 2 * k + half, w_send.at[half, way], target)
+
+    def w_sib(group, half):
+        return w_push(other_w, block_of(4 * group) + 2 * k + half, w_sib_send.at[group, half], sibling)
+
+    def w_wait(b):
+        w_push(other_w, b, w_send.at[0, 0], sibling).wait_recv()
+
+    def w_spread(half):
+        w_wait(4 * x + 2 * k + half)
+        for way in range(4):
+            w_side(half, way).start()
+
+    def w_hand_over(group):
+        for half in range(2):
+            w_wait(block_of(4 * group) + 2 * k + half)
+            w_sib(group, half).start()
 
     spread(0)
     for d in range(1, SEQ):
         landed(qr, q_recv, (s + d) % SEQ)
     qt[...] = jnp.transpose(qr[...].reshape(QROWS, HD).astype(F32)).astype(BF16)
-    for b in range(CHUNKS):
+    for b in range(BLOCKS):
         load_own(b).wait()
 
-    @pl.when(z == 0)
+    @pl.when(z % 3 == 0)
     def _():
-        def origin(u, carry):
-            w_push(u, True, below).start()
-            return carry
-
-        lax.fori_loop(0, DOWN, origin, 0)
+        for half in range(2):
+            for hop in (1, 2):
+                w_edge(half, hop).start()
 
     own_pair = z * 4 + x
 
@@ -236,7 +243,9 @@
             acc[:, cols] = acc[:, cols] * factor + update[:HD]
             ready = ahead
 
-    first_relay = 8 - 2 * z
+    def pass_on(t):
+        wait_slot(column_slot(t))
+        spread(t)
 
     def step(n, carry):
         t, i = n // 4, n % 4
@@ -247,17 +256,17 @@
         def _():
             attend(pair)
 
-        @pl.when((i == 0) & (t < z))
-        def _():
-            wait_slot(column_slot(t + 1))
-            spread(t + 1)
-
         @pl.when(n == 0)
         def _():
             from_beside(0, 0)
             from_beside(0, 1)
 
-        @pl.when(i == 1)
+        for ahead, at in ((1, 0), (2, 2), (3, 5)):
+            @pl.when((n == at) & (z >= ahead))
+            def _(ahead=ahead):
+                pass_on(ahead)
+
+        @pl.when((n == 2) | ((i == 1) & (t > 0)))
         def _():
             from_across(t)
 
@@ -266,13 +275,13 @@
             from_beside(t + 1, 0)
             from_beside(t + 1, 1)
 
-        @pl.when((z == 3) & (n < CHUNKS - DOWN))
-        def _():
-            w_push(DOWN + n, True, above).start()
-
-        @pl.when((n >= first_relay) & (n % 2 == 0) & (n < first_relay + 2 * DOWN))
-        def _():
-            w_relay((n - first_relay) // 2, 0, below)
+        @pl.when(n == 4 * z + 1 - 4 * (z // 3))
+        def _():
+            w_spread(0)
+
+        @pl.when(n == 4 * z + 3 - 2 * (z // 3))
+        def _():
+            w_spread(1)
 
         return carry
 
@@ -283,19 +292,6 @@
     att[...] = out.reshape(SEQ, GROUP, ROWS, HD)
     swap = push(att.at[pl.ds(4 * (1 - zh), 4)], att_in, swap_sem.at[0], swap_sem.at[1], partner)
     swap.start()
-
-    def late(u, carry):
-        @pl.when(u >= (6 * z - 3) // 2)
-        def _():
-            w_relay(u, 0, below)
-
-        @pl.when(u < CHUNKS - DOWN)
-        def _():
-            w_relay(DOWN + u, 3, above)
-
-        return carry
-
-    lax.fori_loop(0, DOWN, late, 0)
 
     def gather_rows(source, first, place):
         for h in range(GROUP):
@@ -315,17 +311,23 @@
         return (y + 1 + hop) % 4 if dirn else (y + 3 - hop) % 4
 
     def first(j, carry):
-        for b in range(4):
-            w_from = w_slice(other_w, 1 - k, 4 * j + b)
-            push(w_from, w_from, w_sib_send.at[0], w_recv.at[1 - k, 4 * j + b], sibling).wait_recv()
+        @pl.when(j % 2 != k)
+        def _():
+            for dirn in range(2):
+                w_wait(block_of(2 * j + dirn))
+
         for dirn in range(2):
-            q = dirn * NC + j
-            for b in range(2):
-                product = jnp.dot(rows_in[0], own_w[2 * q + b], preferred_element_type=F32)
-                product += jnp.dot(rows_in[1], other_w[2 * q + b], preferred_element_type=F32)
-                part[q, :, :, b * CT : (b + 1) * CT] = product.reshape(4, ROWS, CT)
-            sends[0, dirn, j] = part[q, block_at(0, dirn)].astype(BF16)
+            q = block_of(2 * j + dirn)
+            product = jnp.dot(rows_in[0], own_w[q], preferred_element_type=F32)
+            product += jnp.dot(rows_in[1], other_w[q], preferred_element_type=F32)
+            part[dirn, j] = product.reshape(4, ROWS, CT)
+            sends[0, dirn, j] = part[dirn, j, block_at(0, dirn)].astype(BF16)
             ring(0, dirn, j).start()
+
+        @pl.when((j % 2 == 0) & (j < 6))
+        def _():
+            w_hand_over(j // 2 + 1)
+
         return carry
 
     lax.fori_loop(0, NC, first, 0)
@@ -333,10 +335,9 @@
     for hop in (1, 2):
         def middle(j, carry, hop=hop):
             for dirn in range(2):
-                q = dirn * NC + j
                 ring(hop - 1, dirn, j).wait_recv()
                 sends[hop, dirn, j] = (
-                    recvs[hop - 1, dirn, j].astype(F32) + part[q, block_at(hop, dirn)]
+                    recvs[hop - 1, dirn, j].astype(F32) + part[dirn, j, block_at(hop, dirn)]
                 ).astype(BF16)
                 ring(hop, dirn, j).start()
             return carry
@@ -347,19 +348,21 @@
     load_gate.wait()
     level = level_ref[c]
 
-    def final(q):
-        cols = pl.ds(pl.multiple_of(q * CW, CW), CW)
-        return push(done.at[:, cols], out_ref.at[:, cols], out_send.at[q], out_recv.at[q], after)
+    def columns(place):
+        return pl.ds(pl.multiple_of(block_of(place) * CT, CT), CT)
+
+    def final(place):
+        cols = columns(place)
+        return push(done.at[:, cols], out_ref.at[:, cols], out_send.at[place], out_recv.at[place], after)
 
     def last(j, carry):
         for dirn in range(2):
-            q = dirn * NC + j
-            cols = pl.ds(pl.multiple_of(q * CW, CW), CW)
+            cols = columns(2 * j + dirn)
             ring(2, dirn, j).wait_recv()
-            branch = recvs[2, dirn, j].astype(F32) + part[q, y]
+            branch = recvs[2, dirn, j].astype(F32) + part[dirn, j, y]
             gate_row = gate[pl.ds(level, 1), cols]
             done[:, cols] = (lat[:, cols].astype(F32) + gate_row * branch).astype(BF16)
-            final(q).start()
+            final(2 * j + dirn).start()
         return carry
 
     lax.fori_loop(0, NC, last, 0)
@@ -382,21 +385,27 @@
         sib_copy(n).wait_send()
         return carry
 
-    def drain_w(u, carry):
-        w_push(u, False, below).wait_send()
-        w_sib(u).wait_send()
-        return carry
+    @pl.when(z % 3 == 0)
+    def _():
+        for half in range(2):
+            for hop in (1, 2):
+                w_edge(half, hop).wait_send()
+
+    for half in range(2):
+        for way in range(4):
+            w_side(half, way).wait_send()
+        for group in (1, 2, 3):
+            w_sib(group, half).wait_send()
 
     def drain_ring(j, carry):
         for dirn in range(2):
             for hop in range(3):
                 ring(hop, dirn, j).wait_send()
-            final(dirn * NC + j).wait()
+            final(2 * j + dirn).wait()
         return carry
 
     lax.fori_loop(0, z + 1, drain_plane, 0)
     lax.fori_loop(0, total, drain_sib, 0)
-    lax.fori_loop(0, CHUNKS, drain_w, 0)
     lax.fori_loop(0, NC, drain_ring, 0)
 
 
@@ -421,18 +430,18 @@
             pltpu.VMEM((SEQ, GROUP, ROWS, HD), BF16),
             pltpu.VMEM((4, GROUP, ROWS, HD), BF16),
             pltpu.VMEM((2, 4 * ROWS, CT), BF16),
-            pltpu.VMEM((CHUNKS, CT, CT), BF16),
-            pltpu.VMEM((CHUNKS, CT, CT), BF16),
-            pltpu.VMEM((2 * NC, 4, ROWS, CW), F32),
-            pltpu.VMEM((3, 2, NC, ROWS, CW), BF16),
-            pltpu.VMEM((3, 2, NC, ROWS, CW), BF16),
+            pltpu.VMEM((BLOCKS, CT, CT), BF16),
+            pltpu.VMEM((BLOCKS, CT, CT), BF16),
+            pltpu.VMEM((2, NC, 4, ROWS, CT), F32),
+            pltpu.VMEM((3, 2, NC, ROWS, CT), BF16),
+            pltpu.VMEM((3, 2, NC, ROWS, CT), BF16),
             pltpu.VMEM((ROWS, D), BF16),
             pltpu.VMEM((64, D), F32),
             pltpu.VMEM((ROWS, D), BF16),
             dma((SEQ,)), dma((SEQ,)), dma((SEQ,)), dma((SEQ,)),
             dma((4,)), dma((4, 2)), dma((4, 2)), dma((16,)), dma((32,)), dma((4, 2)),
-            dma((CHUNKS + 2,)), dma((CHUNKS,)), dma((CHUNKS,)), dma((2, CHUNKS)), dma((2,)),
-            dma((3, 2, NC)), dma((3, 2, NC)), dma((2 * NC,)), dma((2 * NC,)),
+            dma((BLOCKS + 2,)), dma((2, 2)), dma((2, 4)), dma((4, 2)), dma((BLOCKS,)), dma((2,)),
+            dma((3, 2, NC)), dma((3, 2, NC)), dma((BLOCKS,)), dma((BLOCKS,)),
         ],
         compiler_params=pltpu.CompilerParams(
             collective_id=0, has_side_effects=True, vmem_limit_bytes=48 * MIB

time: 178 us -> 115 us (0.65)
  Pallas kernels: 169 us -> 107 us
    pallas_call x1, Pallas kernels: 169 us -> 107 us  [fused(): pl.pallas_call(kernel, out_shape=jax.ShapeDtypeStruct((ROWS, D), BF16), i...]
where the time goes in v3:
time: 115 us; the launch traced here: 114 us
  Pallas kernels  107 us (93%)
  local copies, waits for them, and re-layouts  6.62 us (6%)
    pallas_call x1, Pallas kernels, fused(): pl.pallas_call(kernel, out_shape=jax.ShapeDtypeStruct((ROWS, D), BF16), i...  107 us
    unnamed x11, local copies, waits for them, and re-layouts  6.62 us

profile of v3, /device:TPU:8, one launch (start us, length us, event | category | flops | bytes accessed | tf_op | source)
XLA Modules:
  0.0 113.6 jit_solution(14381125329828166961)
XLA Ops:
  0.0 1.0 copy.11
  1.0 1.0 copy.8
  2.0 0.0 copy-start
  2.0 1.4 %copy-done = f32[64,6144]{1,0:T(8,128)S(1)} copy-done((f32[64,6144]{1,0:T(8,128)S(1)}, f32[64,6144]{1,0:T(8,128)}, u32[]{:S(2)}) %copy-start) | copy-done | bytes 1572888
  3.4 0.0 copy-start.1
  3.4 1.1 copy-done.1
  4.4 0.0 copy-start.2
  4.5 0.7 copy-done.2
  5.2 0.0 copy-start.3
  5.2 0.7 copy-done.3
  5.8 106.9 %stretch_attention.1 = bf16[48,6144]{1,0:T(8,128)(2,1)S(1)} custom-call(bf16[8,3,48,128]{3,2,1,0:T(8,128)(2,1)S(1)} %bitcast.6, bf16[8,48,256]{2,1,0:T(8,128)(2,1)S(1)} %bitcast.7, s32[32,32]{1,0:T(8,128)S(1)} %copy-done.2, s32[32]{0:T(128)S(1)} %copy-done.3, bf16[384,6144]{1,0:T(8,128)(2,1)} %own_hbm.1, bf16[48,6144]{1,0:T(8,128)(2,1)S(1)} %copy-done.1, ...), custom_call_target="tpu_custom_call" | custom-call | flops 5435817984 | bytes 20971520 | tf_op jit(solution)/shard_map/stretch_attention/pallas_call | solution.py:417
  112.7 0.8 copy.13
Async XLA Ops:
  2.0 1.4 %copy-start = (f32[64,6144]{1,0:T(8,128)S(1)}, f32[64,6144]{1,0:T(8,128)}, u32[]{:S(2)}) copy-start(f32[64,6144]{1,0:T(8,128)} %gate_hbm.1) | copy-start | bytes 4718596
  3.4 1.1 copy-start.1
  4.4 0.7 copy-start.2
  5.2 0.7 copy-start.3

commit v4 on v3

--- a/solution.py
+++ b/solution.py
@@ -26,8 +26,8 @@
 
 
 def kernel(
-    q_ref, kv_ref, mask_ref, level_ref, own_hbm, lat_hbm, gate_hbm, out_ref,
-    kvr, qr, qt, slots, acc, run_max, run_sum, att, att_in, rows_in,
+    q_raw, kv_raw, mask_hbm, level_hbm, own_hbm, lat_hbm, gate_hbm, out_ref,
+    q_ref, kv_ref, mask_ref, level_ref, kvr, qr, qt, slots, acc, run_max, run_sum, att, att_in, rows_in,
     own_w, other_w, part, sends, recvs, lat, gate, done,
     kv_send, kv_recv, q_send, q_recv, z_send, x_send, relay_send, sib_send, slot_recv, half_recv,
     load_sem, w_edge_send, w_send, w_sib_send, w_recv, swap_sem, ring_send, ring_recv, out_send, out_recv,
@@ -47,7 +47,7 @@
     sibling = dev(z, x, 1 - k)
     above = z_next(1)
     outward = 2 * (z // 3) - 1
-    x_right, x_left, x_across = (dev(z, (x + d) % 4, k) for d in (1, 3, 2))
+    x_right, x_left = dev(z, (x + 1) % 4, k), dev(z, (x + 3) % 4, k)
     partner = (c, (s + 4) % SEQ)
     y_up, y_down = (c, zh * 4 + (y + 1) % 4), (c, zh * 4 + (y + 3) % 4)
     after, before = ((c + 1) % 32, s), ((c + 31) % 32, s)
@@ -62,13 +62,28 @@
 
     load_lat = pltpu.make_async_copy(lat_hbm, lat, load_sem.at[BLOCKS])
     load_gate = pltpu.make_async_copy(gate_hbm, gate, load_sem.at[BLOCKS + 1])
+    load_mask = pltpu.make_async_copy(mask_hbm, mask_ref, load_sem.at[BLOCKS + 2])
+    load_level = pltpu.make_async_copy(level_hbm, level_ref, load_sem.at[BLOCKS + 3])
 
     barrier = pltpu.get_barrier_semaphore()
     greeted = [(c, (s + d) % SEQ) for d in range(1, SEQ)] + [
-        z_next(1), z_next(-1), z_next(2), z_next(-2), x_right, x_left, x_across, sibling, after, before,
+        z_next(1), z_next(-1), x_right, x_left, sibling, after, before,
     ]
     for target in greeted:
         pl.semaphore_signal(barrier, inc=1, device_id=target, device_id_type=MESH)
+    load_mask.start()
+    load_level.start()
+    for b in range(BLOCKS):
+        load_own(b).start()
+    load_lat.start()
+    load_gate.start()
+    kv_ref[...] = jnp.transpose(kv_raw[...], (1, 0, 2))
+    q_ref[...] = jnp.transpose(q_raw[...], (1, 0, 2)).reshape(SEQ, GROUP, ROWS, HD)
+    run_max[...] = jnp.full_like(run_max, -BIG)
+    run_sum[...] = jnp.zeros_like(run_sum)
+    acc[...] = jnp.zeros_like(acc)
+    kvr[s] = kv_ref[s]
+    qr[s] = q_ref[s]
     pl.semaphore_wait(barrier, len(greeted))
 
     def kv_copy(d):
@@ -86,15 +101,6 @@
         kv_copy(d).start()
     for d in (4, 3, 5, 2, 6, 1, 7):
         q_copy(d).start()
-    for b in range(BLOCKS):
-        load_own(b).start()
-    load_lat.start()
-    load_gate.start()
-    kvr[s] = kv_ref[s]
-    qr[s] = q_ref[s]
-    run_max[...] = jnp.full_like(run_max, -BIG)
-    run_sum[...] = jnp.zeros_like(run_sum)
-    acc[...] = jnp.zeros_like(acc)
     for d in range(1, SEQ):
         landed(kvr, kv_recv, (s + d) % SEQ)
     block = kvr[...].reshape(CT, 2 * HD)
@@ -157,37 +163,55 @@
         sib_copy(n).start()
 
     def block_of(place):
-        group = place // 4
-        step = group + group // 2 - 2 * (group // 3)
-        return 4 * ((x + step) % 4) + place % 4
+        return 8 * ((x + place // 8) % 2) + place % 8
 
     def w_push(source, b, send, target):
         return push(source.at[b], other_w.at[b], send, w_recv.at[b], target)
 
-    def w_edge(half, hop):
-        return w_push(own_w, 4 * x + 2 * k + half, w_edge_send.at[half, hop - 1], z_next(hop * outward))
-
-    def w_side(half, way):
-        target = (x_right, x_left, x_across, sibling)[way]
-        return w_push(other_w, 4 * x + 2 * k + half, w_send.at[half, way], target)
-
-    def w_sib(group, half):
-        return w_push(other_w, block_of(4 * group) + 2 * k + half, w_sib_send.at[group, half], sibling)
+    def core_block(b):
+        return block_of(8 * (b // 4) + 4 * ((b // 2) % 2) + 2 * k + b % 2)
+
+    def w_edge(b):
+        return w_push(own_w, core_block(b), w_edge_send.at[b], z_next(outward))
+
+    def w_inward(b):
+        return w_push(other_w, core_block(b), w_send.at[b, 0], z_next(-outward))
+
+    def w_beside(b):
+        return w_push(other_w, core_block(b), w_send.at[b, 1], dev(z, (x + 1 + 2 * (b // 2)) % 4, k))
+
+    def w_sib(b):
+        return w_push(other_w, core_block(b), w_sib_send.at[b], sibling)
 
     def w_wait(b):
-        w_push(other_w, b, w_send.at[0, 0], sibling).wait_recv()
-
-    def w_spread(half):
-        w_wait(4 * x + 2 * k + half)
-        for way in range(4):
-            w_side(half, way).start()
-
-    def w_hand_over(group):
-        for half in range(2):
-            w_wait(block_of(4 * group) + 2 * k + half)
-            w_sib(group, half).start()
+        w_push(other_w, b, w_sib_send.at[0], sibling).wait_recv()
+
+    def w_spread(b):
+        w_wait(core_block(b))
+
+        @pl.when(z % 3 == 0)
+        def _():
+            w_inward(b).start()
+
+        w_beside(b).start()
+        w_sib(b).start()
+
+    def w_hand_over(b):
+        w_wait(core_block(b))
+        w_sib(b).start()
+
+    def pass_on(t):
+        wait_slot(column_slot(t))
+        spread(t)
 
     spread(0)
+    from_beside(0, 0)
+    from_beside(0, 1)
+
+    @pl.when(z >= 1)
+    def _():
+        pass_on(1)
+
     for d in range(1, SEQ):
         landed(qr, q_recv, (s + d) % SEQ)
     qt[...] = jnp.transpose(qr[...].reshape(QROWS, HD).astype(F32)).astype(BF16)
@@ -196,9 +220,11 @@
 
     @pl.when(z % 3 == 0)
     def _():
-        for half in range(2):
-            for hop in (1, 2):
-                w_edge(half, hop).start()
+        for b in range(4):
+            w_edge(b).start()
+
+    load_mask.wait()
+    load_level.wait()
 
     own_pair = z * 4 + x
 
@@ -243,10 +269,6 @@
             acc[:, cols] = acc[:, cols] * factor + update[:HD]
             ready = ahead
 
-    def pass_on(t):
-        wait_slot(column_slot(t))
-        spread(t)
-
     def step(n, carry):
         t, i = n // 4, n % 4
         pair = pair_of(n)
@@ -256,17 +278,12 @@
         def _():
             attend(pair)
 
-        @pl.when(n == 0)
-        def _():
-            from_beside(0, 0)
-            from_beside(0, 1)
-
-        for ahead, at in ((1, 0), (2, 2), (3, 5)):
+        for ahead, at in ((2, 1), (3, 4)):
             @pl.when((n == at) & (z >= ahead))
             def _(ahead=ahead):
                 pass_on(ahead)
 
-        @pl.when((n == 2) | ((i == 1) & (t > 0)))
+        @pl.when(i == 1)
         def _():
             from_across(t)
 
@@ -275,13 +292,13 @@
             from_beside(t + 1, 0)
             from_beside(t + 1, 1)
 
-        @pl.when(n == 4 * z + 1 - 4 * (z // 3))
-        def _():
-            w_spread(0)
-
-        @pl.when(n == 4 * z + 3 - 2 * (z // 3))
-        def _():
-            w_spread(1)
+        @pl.when((z == 3) & (n >= 4) & (n % 3 == 1))
+        def _():
+            w_spread((n - 4) // 3)
+
+        @pl.when((z < 3) & (n >= 4 * z) & (n % 2 == 1))
+        def _():
+            w_spread((n - 4 * z) // 2)
 
         return carry
 
@@ -292,6 +309,11 @@
     att[...] = out.reshape(SEQ, GROUP, ROWS, HD)
     swap = push(att.at[pl.ds(4 * (1 - zh), 4)], att_in, swap_sem.at[0], swap_sem.at[1], partner)
     swap.start()
+
+    @pl.when(z < 3)
+    def _():
+        w_spread(2)
+        w_spread(3)
 
     def gather_rows(source, first, place):
         for h in range(GROUP):
@@ -324,9 +346,10 @@
             sends[0, dirn, j] = part[dirn, j, block_at(0, dirn)].astype(BF16)
             ring(0, dirn, j).start()
 
-        @pl.when((j % 2 == 0) & (j < 6))
-        def _():
-            w_hand_over(j // 2 + 1)
+        @pl.when((j == 1) | (j == 3))
+        def _():
+            w_hand_over(3 + j)
+            w_hand_over(4 + j)
 
         return carry
 
@@ -385,17 +408,15 @@
         sib_copy(n).wait_send()
         return carry
 
-    @pl.when(z % 3 == 0)
-    def _():
-        for half in range(2):
-            for hop in (1, 2):
-                w_edge(half, hop).wait_send()
-
-    for half in range(2):
-        for way in range(4):
-            w_side(half, way).wait_send()
-        for group in (1, 2, 3):
-            w_sib(group, half).wait_send()
+    for b in range(4):
+        @pl.when(z % 3 == 0)
+        def _(b=b):
+            w_edge(b).wait_send()
+            w_inward(b).wait_send()
+
+        w_beside(b).wait_send()
+    for b in range(8):
+        w_sib(b).wait_send()
 
     def drain_ring(j, carry):
         for dirn in range(2):
@@ -409,17 +430,20 @@
     lax.fori_loop(0, NC, drain_ring, 0)
 
 
-def fused(q_t, kv_t, mask, level, own, latents, gate_table):
+def fused(queries, keys_values, mask, level, own, latents, gate_table):
     vmem = pl.BlockSpec(memory_space=pltpu.VMEM)
-    smem = pl.BlockSpec(memory_space=pltpu.SMEM)
     anywhere = pl.BlockSpec(memory_space=pl.ANY)
     dma = pltpu.SemaphoreType.DMA
     return pl.pallas_call(
         kernel,
         out_shape=jax.ShapeDtypeStruct((ROWS, D), BF16),
-        in_specs=[vmem, vmem, smem, smem, anywhere, anywhere, anywhere],
+        in_specs=[vmem, vmem] + [anywhere] * 5,
         out_specs=vmem,
         scratch_shapes=[
+            pltpu.VMEM((SEQ, GROUP, ROWS, HD), BF16),
+            pltpu.VMEM((SEQ, ROWS, 2 * HD), BF16),
+            pltpu.SMEM((32, 32), jnp.int32),
+            pltpu.SMEM((32,), jnp.int32),
             pltpu.VMEM((SEQ, ROWS, 2 * HD), BF16),
             pltpu.VMEM((SEQ, GROUP, ROWS, HD), BF16),
             pltpu.VMEM((HD, QROWS), BF16),
@@ -440,23 +464,21 @@
             pltpu.VMEM((ROWS, D), BF16),
             dma((SEQ,)), dma((SEQ,)), dma((SEQ,)), dma((SEQ,)),
             dma((4,)), dma((4, 2)), dma((4, 2)), dma((16,)), dma((32,)), dma((4, 2)),
-            dma((BLOCKS + 2,)), dma((2, 2)), dma((2, 4)), dma((4, 2)), dma((BLOCKS,)), dma((2,)),
+            dma((BLOCKS + 4,)), dma((4,)), dma((4, 2)), dma((8,)), dma((BLOCKS,)), dma((2,)),
             dma((3, 2, NC)), dma((3, 2, NC)), dma((BLOCKS,)), dma((BLOCKS,)),
         ],
         compiler_params=pltpu.CompilerParams(
-            collective_id=0, has_side_effects=True, vmem_limit_bytes=48 * MIB
+            collective_id=0, has_side_effects=True, vmem_limit_bytes=60 * MIB
         ),
         cost_estimate=pl.CostEstimate(
             flops=4 * QROWS * HD * CT * 24, bytes_accessed=20 * MIB, transcendentals=QROWS * CT * 24
         ),
         name="stretch_attention",
-    )(q_t, kv_t, mask, level, own, latents, gate_table)
+    )(queries, keys_values, mask, level, own, latents, gate_table)
 
 
 def on_device(queries, keys_values, out_weight, latents, gate_table, noise_level, stretch_mask):
-    q_t = jnp.transpose(queries.reshape(ROWS, SEQ, GROUP, HD), (1, 2, 0, 3))
-    kv_t = jnp.transpose(keys_values, (1, 0, 2))
-    return fused(q_t, kv_t, stretch_mask, noise_level, out_weight, latents, gate_table)
+    return fused(queries, keys_values, stretch_mask, noise_level, out_weight, latents, gate_table)
 
 
 def solution(mesh):

time: 115 us -> 112 us (0.974)
  local copies, waits for them, and re-layouts: 6.62 us -> 1.92 us
  Pallas kernels: 107 us -> 109 us
    unnamed x11 -> x1, local copies, waits for them, and re-layouts: 6.62 us -> 1.92 us
    pallas_call x1, Pallas kernels: 107 us -> 109 us  [fused(): pl.pallas_call(kernel, out_shape=jax.ShapeDtypeStruct((ROWS, D), BF16), i...]
where the time goes in v4:
time: 112 us; the launch traced here: 111 us
  Pallas kernels  109 us (97%)
  local copies, waits for them, and re-layouts  1.92 us (2%)
    pallas_call x1, Pallas kernels, fused(): pl.pallas_call(kernel, out_shape=jax.ShapeDtypeStruct((ROWS, D), BF16), i...  109 us

profile of v4, /device:TPU:8, one launch (start us, length us, event | category | flops | bytes accessed | tf_op | source)
XLA Modules:
  0.0 111.0 jit_solution(16316958332489897727)
XLA Ops:
  0.0 109.1 %stretch_attention.1 = bf16[48,6144]{1,0:T(8,128)(2,1)} custom-call(bf16[48,24,128]{2,1,0:T(8,128)(2,1)} %q_raw.1, bf16[48,8,256]{2,1,0:T(8,128)(2,1)} %kv_raw.1, s32[32,32]{1,0:T(8,128)} %mask_hbm.1, s32[32]{0:T(128)} %level_hbm.1, bf16[384,6144]{1,0:T(8,128)(2,1)} %own_hbm.1, bf16[48,6144]{1,0:T(8,128)(2,1)} %lat_hbm.1, f32[64,6144]{1,0:T(8,128)} %gate_hbm.1), custom_call_target="tpu_custom_call" | custom-call | flops 5435817984 | bytes 20971520 | tf_op jit(solution)/shard_map/stretch_attention/pallas_call | solution.py:437
  109.1 1.9 %copy.9 = bf16[48,6144]{1,0:T(8,128)(2,1)} copy(bf16[48,6144]{1,0:T(8,128)(2,1)} %stretch_attention.1) | data formatting | bytes 1179648

commit v5 on v4

--- a/solution.py
+++ b/solution.py
@@ -22,20 +22,23 @@
 EXP_SCALE = math.log2(math.e) / math.sqrt(HD)
 
 NC = 8
+LAG = 2
 BLOCKS = 16
 
 
 def kernel(
     q_raw, kv_raw, mask_hbm, level_hbm, own_hbm, lat_hbm, gate_hbm, out_ref,
-    q_ref, kv_ref, mask_ref, level_ref, kvr, qr, qt, slots, acc, run_max, run_sum, att, att_in, rows_in,
+    q_ref, kv_ref, mask_ref, level_ref, q_far, att_far, mate_att, blend, lse, lse_partner, lse_mate, kvr, qr, qt, slots, acc, run_max, run_sum, att, att_in, rows_in,
     own_w, other_w, part, sends, recvs, lat, gate, done,
-    kv_send, kv_recv, q_send, q_recv, z_send, x_send, relay_send, sib_send, slot_recv, half_recv,
+    mate_send, mate_recv, kv_send, kv_recv, q_send, q_recv, z_send, down_send, x_send, relay_send, sib_send, slot_recv, half_recv,
     load_sem, w_edge_send, w_send, w_sib_send, w_recv, swap_sem, ring_send, ring_recv, out_send, out_recv,
 ):
     c = lax.axis_index("stretch")
     s = lax.axis_index("seq")
     z, x, k = c // 8, (c // 2) % 4, c % 2
     zh, y = s // 4, s % 4
+    bottom = 1 - (z + 3) // 4
+    planes = 2 + z // 2 - z // 3
 
     def dev(zz, xx, kk):
         return ((zz * 4 + xx) * 2 + kk, s)
@@ -47,7 +50,8 @@
     sibling = dev(z, x, 1 - k)
     above = z_next(1)
     outward = 2 * (z // 3) - 1
-    x_right, x_left = dev(z, (x + 1) % 4, k), dev(z, (x + 3) % 4, k)
+    mate = dev(3 - z, x, k)
+    x_right, x_left, x_across = (dev(z, (x + d) % 4, k) for d in (1, 3, 2))
     partner = (c, (s + 4) % SEQ)
     y_up, y_down = (c, zh * 4 + (y + 1) % 4), (c, zh * 4 + (y + 3) % 4)
     after, before = ((c + 1) % 32, s), ((c + 31) % 32, s)
@@ -67,7 +71,8 @@
 
     barrier = pltpu.get_barrier_semaphore()
     greeted = [(c, (s + d) % SEQ) for d in range(1, SEQ)] + [
-        z_next(1), z_next(-1), x_right, x_left, sibling, after, before,
+        z_next(1), z_next(-1), x_right, x_left, x_across, sibling, mate,
+        after, before,
     ]
     for target in greeted:
         pl.semaphore_signal(barrier, inc=1, device_id=target, device_id_type=MESH)
@@ -99,8 +104,6 @@
 
     for d in (4, 3, 5, 2, 6, 1, 7):
         kv_copy(d).start()
-    for d in (4, 3, 5, 2, 6, 1, 7):
-        q_copy(d).start()
     for d in range(1, SEQ):
         landed(kvr, kv_recv, (s + d) % SEQ)
     block = kvr[...].reshape(CT, 2 * HD)
@@ -112,8 +115,11 @@
     def slot_push(j, send, target):
         return push(slots.at[j], slots.at[j], send, slot_recv.at[j], target)
 
+    def plane_of(t):
+        return z - t + 2 * t * bottom
+
     def column_slot(t):
-        return ((z - t) * 4 + x) * 2 + k
+        return (plane_of(t) * 4 + x) * 2 + k
 
     def z_copy(t):
         return slot_push(column_slot(t), z_send.at[t], above)
@@ -124,7 +130,7 @@
     def pair_of(n):
         t, i = n // 4, n % 4
         step = i + i // 2 - 2 * (i // 3)
-        return (z - t) * 4 + (x + step) % 4
+        return plane_of(t) * 4 + (x + step) % 4
 
     def sib_copy(n):
         return slot_push(2 * pair_of(n) + k, sib_send.at[n], sibling)
@@ -136,15 +142,22 @@
         )
 
     def relay(t, right):
-        return half_of(t, (z - t) * 4 + (x + 1 + 2 * right) % 4, right)
+        return half_of(t, plane_of(t) * 4 + (x + 1 + 2 * right) % 4, right)
 
     def wait_slot(j):
         slot_push(j, z_send.at[0], sibling).wait_recv()
 
+    def down_copy():
+        return slot_push(column_slot(0), down_send.at[0], z_next(-1))
+
     def spread(t):
-        @pl.when(z < 3)
+        @pl.when((z == 1) | ((z % 2 == 0) & (t == 0)))
         def _():
             z_copy(t).start()
+
+        @pl.when((z == 1) & (t == 0))
+        def _():
+            down_copy().start()
 
         x_copy(t, 0).start()
         x_copy(t, 1).start()
@@ -163,13 +176,15 @@
         sib_copy(n).start()
 
     def block_of(place):
-        return 8 * ((x + place // 8) % 2) + place % 8
+        group = place // 4
+        step = group + group // 2 - 2 * (group // 3)
+        return 4 * ((x + step) % 4) + place % 4
 
     def w_push(source, b, send, target):
         return push(source.at[b], other_w.at[b], send, w_recv.at[b], target)
 
     def core_block(b):
-        return block_of(8 * (b // 4) + 4 * ((b // 2) % 2) + 2 * k + b % 2)
+        return block_of(4 * (b // 2) + 2 * k + b % 2)
 
     def w_edge(b):
         return w_push(own_w, core_block(b), w_edge_send.at[b], z_next(outward))
@@ -177,8 +192,9 @@
     def w_inward(b):
         return w_push(other_w, core_block(b), w_send.at[b, 0], z_next(-outward))
 
-    def w_beside(b):
-        return w_push(other_w, core_block(b), w_send.at[b, 1], dev(z, (x + 1 + 2 * (b // 2)) % 4, k))
+    def w_beside(b, way):
+        target = (x_right, x_left, x_across)[way]
+        return w_push(other_w, core_block(b), w_send.at[b, 1 + way], target)
 
     def w_sib(b):
         return w_push(other_w, core_block(b), w_sib_send.at[b], sibling)
@@ -193,7 +209,8 @@
         def _():
             w_inward(b).start()
 
-        w_beside(b).start()
+        for way in range(3):
+            w_beside(b, way).start()
         w_sib(b).start()
 
     def w_hand_over(b):
@@ -205,33 +222,58 @@
         spread(t)
 
     spread(0)
+    for d in (4, 3, 5, 2, 6, 1, 7):
+        q_copy(d).start()
     from_beside(0, 0)
     from_beside(0, 1)
 
-    @pl.when(z >= 1)
-    def _():
-        pass_on(1)
+    pass_on(1)
 
     for d in range(1, SEQ):
         landed(qr, q_recv, (s + d) % SEQ)
-    qt[...] = jnp.transpose(qr[...].reshape(QROWS, HD).astype(F32)).astype(BF16)
+    q_mate = push(qr, q_far, mate_send.at[0], mate_recv.at[0], mate)
+
+    @pl.when(z == 3)
+    def _():
+        q_mate.start()
+
+    def take_queries(source):
+        qt[...] = jnp.transpose(source[...].reshape(QROWS, HD).astype(F32)).astype(BF16)
+
+    take_queries(qr)
     for b in range(BLOCKS):
         load_own(b).wait()
 
     @pl.when(z % 3 == 0)
     def _():
-        for b in range(4):
+        for b in range(2):
             w_edge(b).start()
 
     load_mask.wait()
     load_level.wait()
 
     own_pair = z * 4 + x
-
-    def attend(pair):
+    swap = push(att.at[pl.ds(4 * (1 - zh), 4)], att_in, swap_sem.at[0], swap_sem.at[1], partner)
+    lse_swap = push(lse, lse_partner, mate_send.at[1], mate_recv.at[1], partner)
+
+    def mate_part(near, target):
+        half = zh if near else 1 - zh
+        at = 0 if near else 1
+        return (
+            push(att_far.at[pl.ds(4 * half, 4)], mate_att.at[at], mate_send.at[2 + at], mate_recv.at[2 + at], target),
+            push(lse, lse_mate.at[at], mate_send.at[4 + at], mate_recv.at[4 + at], target),
+        )
+
+    def finish(target):
+        total_weight = jnp.maximum(run_sum[...], 1e-30)
+        out = jnp.transpose(acc[...] * (1.0 / total_weight)).astype(BF16)
+        target[...] = out.reshape(SEQ, GROUP, ROWS, HD)
+        lse[...] = jnp.broadcast_to(run_max[...] * EXP_SCALE + jnp.log2(total_weight), lse.shape)
+
+    def attend(pair, row):
         ja = 2 * pair
-        hide_a = jnp.where(mask_ref[c, ja] == 1, 0.0, BIG).astype(F32)
-        hide_b = jnp.where(mask_ref[c, ja + 1] == 1, 0.0, BIG).astype(F32)
+        hide_a = jnp.where(mask_ref[row, ja] == 1, 0.0, 2 * BIG).astype(F32)
+        hide_b = jnp.where(mask_ref[row, ja + 1] == 1, 0.0, 2 * BIG).astype(F32)
         ones = jnp.ones((16, CT), BF16)
 
         def values(j):
@@ -269,58 +311,100 @@
             acc[:, cols] = acc[:, cols] * factor + update[:HD]
             ready = ahead
 
+    w_first = jnp.where(z == 2, 8, 3)
+    w_count = jnp.where(z == 1, 0, 2)
+
     def step(n, carry):
-        t, i = n // 4, n % 4
-        pair = pair_of(n)
-        wait_slot(2 * pair + 1 - k)
-
-        @pl.when(pair <= own_pair)
-        def _():
-            attend(pair)
-
-        for ahead, at in ((2, 1), (3, 4)):
-            @pl.when((n == at) & (z >= ahead))
-            def _(ahead=ahead):
-                pass_on(ahead)
-
-        @pl.when(i == 1)
+        t, i = (n // 4) // (1 + bottom), n % 4
+        fresh = (bottom == 0) | (n // 4 != 1)
+        for_mate = (bottom == 1) & (n >= 4)
+        pair = pair_of(4 * t + i)
+
+        @pl.when((bottom == 1) & (n == 4))
+        def _():
+            finish(att)
+            swap.start()
+            q_mate.wait_recv()
+            take_queries(q_far)
+            run_max[...] = jnp.full_like(run_max, -BIG)
+            run_sum[...] = jnp.zeros_like(run_sum)
+            acc[...] = jnp.zeros_like(acc)
+
+        @pl.when(fresh)
+        def _():
+            wait_slot(2 * pair + 1 - k)
+
+        @pl.when((pair <= own_pair) | for_mate)
+        def _():
+            attend(pair, c + 24 * bottom * ((n + 8) // 12))
+
+        @pl.when((n == 1) & (z == 2))
+        def _():
+            pass_on(2)
+
+        @pl.when((i == 1) & fresh)
         def _():
             from_across(t)
 
-        @pl.when((i == 3) & (t < z))
-        def _():
-            from_beside(t + 1, 0)
-            from_beside(t + 1, 1)
-
-        @pl.when((z == 3) & (n >= 4) & (n % 3 == 1))
-        def _():
-            w_spread((n - 4) // 3)
-
-        @pl.when((z < 3) & (n >= 4 * z) & (n % 2 == 1))
-        def _():
-            w_spread((n - 4 * z) // 2)
+        @pl.when((i == 3) & (n // 4 + 1 < planes))
+        def _():
+            from_beside(n // 4 + 1, 0)
+            from_beside(n // 4 + 1, 1)
+
+        turn = n - w_first
+
+        @pl.when((turn >= 0) & (turn % 3 == 0) & (turn < 3 * w_count))
+        def _():
+            w_spread(turn // 3)
 
         return carry
 
-    total = 4 * (z + 1)
-    lax.fori_loop(0, total, step, 0)
-
-    out = jnp.transpose(acc[...] * (1.0 / run_sum[...])).astype(BF16)
-    att[...] = out.reshape(SEQ, GROUP, ROWS, HD)
-    swap = push(att.at[pl.ds(4 * (1 - zh), 4)], att_in, swap_sem.at[0], swap_sem.at[1], partner)
-    swap.start()
-
-    @pl.when(z < 3)
-    def _():
-        w_spread(2)
-        w_spread(3)
+    lax.fori_loop(0, 4 * (planes + bottom), step, 0)
+
+    @pl.when(z == 0)
+    def _():
+        finish(att_far)
+        for copy in mate_part(True, mate) + mate_part(False, z_next(-1)):
+            copy.start()
+
+    @pl.when(z != 0)
+    def _():
+        finish(att)
+        swap.start()
+
+    @pl.when(z == 3)
+    def _():
+        lse_swap.start()
+
+    @pl.when(w_count == 0)
+    def _():
+        w_spread(0)
+        w_spread(1)
 
     def gather_rows(source, first, place):
         for h in range(GROUP):
             rows_in[place, :, h * HD : (h + 1) * HD] = source[pl.ds(first, 4), h].reshape(4 * ROWS, HD)
 
+    def blended(near, lse_home, lse_far, home, far):
+        top = jnp.maximum(lse_home, lse_far)
+        home_weight, far_weight = jnp.exp2(lse_home - top), jnp.exp2(lse_far - top)
+        share = jnp.broadcast_to(home_weight / (home_weight + far_weight), (HD, QROWS))
+        blend[...] = jnp.transpose(share).reshape(SEQ, GROUP, ROWS, HD)
+        part_of = blend[pl.ds(4 * zh, 4)]
+        mixed = part_of * home.astype(F32) + (1.0 - part_of) * far.astype(F32)
+        return mixed.astype(BF16)
+
+    swap.wait()
+
+    @pl.when(z == 3)
+    def _():
+        lse_swap.wait()
+        for copy in mate_part(True, mate) + mate_part(False, mate):
+            copy.wait_recv()
+        att[pl.ds(4 * zh, 4)] = blended(True, lse[0:1], lse_mate[0, 0:1], att[pl.ds(4 * zh, 4)], mate_att[0])
+        att_in[...] = blended(False, lse_partner[0:1], lse_mate[1, 0:1], att_in[...], mate_att[1])
+
     gather_rows(att, 4 * zh, 0)
-    swap.wait()
     gather_rows(att_in, 0, 1)
 
     def ring(hop, dirn, j):
@@ -332,7 +416,18 @@
     def block_at(hop, dirn):
         return (y + 1 + hop) % 4 if dirn else (y + 3 - hop) % 4
 
-    def first(j, carry):
+    def columns(place):
+        return pl.ds(pl.multiple_of(block_of(place) * CT, CT), CT)
+
+    def final(place):
+        cols = columns(place)
+        return push(done.at[:, cols], out_ref.at[:, cols], out_send.at[place], out_recv.at[place], after)
+
+    load_lat.wait()
+    load_gate.wait()
+    level = level_ref[c]
+
+    def first(j):
         @pl.when(j % 2 != k)
         def _():
             for dirn in range(2):
@@ -346,39 +441,15 @@
             sends[0, dirn, j] = part[dirn, j, block_at(0, dirn)].astype(BF16)
             ring(0, dirn, j).start()
 
-        @pl.when((j == 1) | (j == 3))
-        def _():
-            w_hand_over(3 + j)
-            w_hand_over(4 + j)
-
-        return carry
-
-    lax.fori_loop(0, NC, first, 0)
-
-    for hop in (1, 2):
-        def middle(j, carry, hop=hop):
-            for dirn in range(2):
-                ring(hop - 1, dirn, j).wait_recv()
-                sends[hop, dirn, j] = (
-                    recvs[hop - 1, dirn, j].astype(F32) + part[dirn, j, block_at(hop, dirn)]
-                ).astype(BF16)
-                ring(hop, dirn, j).start()
-            return carry
-
-        lax.fori_loop(0, NC, middle, 0)
-
-    load_lat.wait()
-    load_gate.wait()
-    level = level_ref[c]
-
-    def columns(place):
-        return pl.ds(pl.multiple_of(block_of(place) * CT, CT), CT)
-
-    def final(place):
-        cols = columns(place)
-        return push(done.at[:, cols], out_ref.at[:, cols], out_send.at[place], out_recv.at[place], after)
-
-    def last(j, carry):
+    def middle(hop, j):
+        for dirn in range(2):
+            ring(hop - 1, dirn, j).wait_recv()
+            sends[hop, dirn, j] = (
+                recvs[hop - 1, dirn, j].astype(F32) + part[dirn, j, block_at(hop, dirn)]
+            ).astype(BF16)
+            ring(hop, dirn, j).start()
+
+    def last(j):
         for dirn in range(2):
             cols = columns(2 * j + dirn)
             ring(2, dirn, j).wait_recv()
@@ -386,16 +457,36 @@
             gate_row = gate[pl.ds(level, 1), cols]
             done[:, cols] = (lat[:, cols].astype(F32) + gate_row * branch).astype(BF16)
             final(2 * j + dirn).start()
+
+    def tick(tau, carry):
+        @pl.when(tau >= 3 * LAG)
+        def _():
+            last(tau - 3 * LAG)
+
+        for hop in (2, 1):
+            @pl.when((tau >= hop * LAG) & (tau < NC + hop * LAG))
+            def _(hop=hop):
+                middle(hop, tau - hop * LAG)
+
+        @pl.when(tau < NC)
+        def _():
+            first(tau)
+
+        @pl.when((tau < 6) & (tau % 2 == 1))
+        def _():
+            w_hand_over(tau + 1)
+            w_hand_over(tau + 2)
+
         return carry
 
-    lax.fori_loop(0, NC, last, 0)
+    lax.fori_loop(0, NC + 3 * LAG, tick, 0)
 
     for d in range(1, SEQ):
         kv_copy(d).wait_send()
         q_copy(d).wait_send()
 
     def drain_plane(t, carry):
-        @pl.when(z < 3)
+        @pl.when((z == 1) | ((z % 2 == 0) & (t == 0)))
         def _():
             z_copy(t).wait_send()
 
@@ -404,17 +495,31 @@
             relay(t, right).wait_send()
         return carry
 
+    @pl.when(z == 1)
+    def _():
+        down_copy().wait_send()
+
+    @pl.when(z == 0)
+    def _():
+        for copy in mate_part(True, mate) + mate_part(False, z_next(-1)):
+            copy.wait_send()
+
+    @pl.when(z == 3)
+    def _():
+        q_mate.wait_send()
+
     def drain_sib(n, carry):
         sib_copy(n).wait_send()
         return carry
 
-    for b in range(4):
+    for b in range(2):
         @pl.when(z % 3 == 0)
         def _(b=b):
             w_edge(b).wait_send()
             w_inward(b).wait_send()
 
-        w_beside(b).wait_send()
+        for way in range(3):
+            w_beside(b, way).wait_send()
     for b in range(8):
         w_sib(b).wait_send()
 
@@ -425,8 +530,8 @@
             final(2 * j + dirn).wait()
         return carry
 
-    lax.fori_loop(0, z + 1, drain_plane, 0)
-    lax.fori_loop(0, total, drain_sib, 0)
+    lax.fori_loop(0, planes, drain_plane, 0)
+    lax.fori_loop(0, 4 * planes, drain_sib, 0)
     lax.fori_loop(0, NC, drain_ring, 0)
 
 
@@ -438,12 +543,19 @@
         kernel,
         out_shape=jax.ShapeDtypeStruct((ROWS, D), BF16),
         in_specs=[vmem, vmem] + [anywhere] * 5,
-        out_specs=vmem,
+        out_specs=anywhere,
         scratch_shapes=[
             pltpu.VMEM((SEQ, GROUP, ROWS, HD), BF16),
             pltpu.VMEM((SEQ, ROWS, 2 * HD), BF16),
             pltpu.SMEM((32, 32), jnp.int32),
             pltpu.SMEM((32,), jnp.int32),
+            pltpu.VMEM((SEQ, GROUP, ROWS, HD), BF16),
+            pltpu.VMEM((SEQ, GROUP, ROWS, HD), BF16),
+            pltpu.VMEM((2, 4, GROUP, ROWS, HD), BF16),
+            pltpu.VMEM((SEQ, GROUP, ROWS, HD), F32),
+            pltpu.VMEM((8, QROWS), F32),
+            pltpu.VMEM((8, QROWS), F32),
+            pltpu.VMEM((2, 8, QROWS), F32),
             pltpu.VMEM((SEQ, ROWS, 2 * HD), BF16),
             pltpu.VMEM((SEQ, GROUP, ROWS, HD), BF16),
             pltpu.VMEM((HD, QROWS), BF16),
@@ -462,9 +574,9 @@
             pltpu.VMEM((ROWS, D), BF16),
             pltpu.VMEM((64, D), F32),
             pltpu.VMEM((ROWS, D), BF16),
-            dma((SEQ,)), dma((SEQ,)), dma((SEQ,)), dma((SEQ,)),
-            dma((4,)), dma((4, 2)), dma((4, 2)), dma((16,)), dma((32,)), dma((4, 2)),
-            dma((BLOCKS + 4,)), dma((4,)), dma((4, 2)), dma((8,)), dma((BLOCKS,)), dma((2,)),
+            dma((6,)), dma((6,)), dma((SEQ,)), dma((SEQ,)), dma((SEQ,)), dma((SEQ,)),
+            dma((4,)), dma((1,)), dma((4, 2)), dma((4, 2)), dma((16,)), dma((32,)), dma((4, 2)),
+            dma((BLOCKS + 4,)), dma((2,)), dma((2, 4)), dma((8,)), dma((BLOCKS,)), dma((2,)),
             dma((3, 2, NC)), dma((3, 2, NC)), dma((BLOCKS,)), dma((BLOCKS,)),
         ],
         compiler_params=pltpu.CompilerParams(

time: 112 us -> 110 us (0.982)
  the two profiles are of different devices: /device:TPU:8 before, /device:TPU:64 now
where the time goes in v5:
time: 110 us
  Pallas kernels  108 us (98%)
  local copies, waits for them, and re-layouts  1.92 us (2%)
    pallas_call x1, Pallas kernels, fused(): pl.pallas_call(kernel, out_shape=jax.ShapeDtypeStruct((ROWS, D), BF16), i...  108 us

profile of v5, /device:TPU:64, one launch (start us, length us, event | category | flops | bytes accessed | tf_op | source)
XLA Modules:
  0.0 109.6 jit_solution(9922415476514550380)
XLA Ops:
  0.0 107.7 %stretch_attention.1 = bf16[48,6144]{1,0:T(8,128)(2,1)} custom-call(bf16[48,24,128]{2,1,0:T(8,128)(2,1)} %q_raw.1, bf16[48,8,256]{2,1,0:T(8,128)(2,1)} %kv_raw.1, s32[32,32]{1,0:T(8,128)} %mask_hbm.1, s32[32]{0:T(128)} %level_hbm.1, bf16[384,6144]{1,0:T(8,128)(2,1)} %own_hbm.1, bf16[48,6144]{1,0:T(8,128)(2,1)} %lat_hbm.1, f32[64,6144]{1,0:T(8,128)} %gate_hbm.1), custom_call_target="tpu_custom_call" | custom-call | flops 5435817984 | bytes 20971520 | tf_op jit(solution)/shard_map/stretch_attention/pallas_call | solution.py:542
  107.7 1.9 %copy.9 = bf16[48,6144]{1,0:T(8,128)(2,1)} copy(bf16[48,6144]{1,0:T(8,128)(2,1)} %stretch_attention.1) | data formatting | bytes 1179648

commit v6 on v5

--- a/solution.py
+++ b/solution.py
@@ -22,7 +22,6 @@
 EXP_SCALE = math.log2(math.e) / math.sqrt(HD)
 
 NC = 8
-LAG = 2
 BLOCKS = 16
 
 
@@ -51,7 +50,7 @@
     above = z_next(1)
     outward = 2 * (z // 3) - 1
     mate = dev(3 - z, x, k)
-    x_right, x_left, x_across = (dev(z, (x + d) % 4, k) for d in (1, 3, 2))
+    x_right, x_left = dev(z, (x + 1) % 4, k), dev(z, (x + 3) % 4, k)
     partner = (c, (s + 4) % SEQ)
     y_up, y_down = (c, zh * 4 + (y + 1) % 4), (c, zh * 4 + (y + 3) % 4)
     after, before = ((c + 1) % 32, s), ((c + 31) % 32, s)
@@ -71,8 +70,7 @@
 
     barrier = pltpu.get_barrier_semaphore()
     greeted = [(c, (s + d) % SEQ) for d in range(1, SEQ)] + [
-        z_next(1), z_next(-1), x_right, x_left, x_across, sibling, mate,
-        after, before,
+        z_next(1), z_next(-1), x_right, x_left, sibling, mate, after, before,
     ]
     for target in greeted:
         pl.semaphore_signal(barrier, inc=1, device_id=target, device_id_type=MESH)
@@ -104,6 +102,62 @@
 
     for d in (4, 3, 5, 2, 6, 1, 7):
         kv_copy(d).start()
+    def block_of(place):
+        group = place // 4
+        step = group + group // 2 - 2 * (group // 3)
+        return 4 * ((x + step) % 4) + place % 4
+
+    def w_push(source, b, send, target):
+        return push(source.at[b], other_w.at[b], send, w_recv.at[b], target)
+
+    def core_block(b):
+        return block_of(4 * (b // 2) + 2 * k + b % 2)
+
+    def w_edge(b):
+        q = core_block(b)
+        return push(own_hbm.at[:, pl.ds(pl.multiple_of(q * CT, CT), CT)], other_w.at[q], w_edge_send.at[b], w_recv.at[q], z_next(outward))
+
+    def w_inward(b):
+        return w_push(other_w, core_block(b), w_send.at[b, 0], z_next(-outward))
+
+    def w_beside(b, way):
+        target = (x_right, x_left)[way]
+        return w_push(other_w, core_block(b), w_send.at[b, 1 + way], target)
+
+    def w_across(half):
+        moved = core_block(2 * (2 - half) + half)
+        return w_push(other_w, moved, w_send.at[half, 3], x_left if half else x_right)
+
+    def w_sib(b):
+        return w_push(other_w, core_block(b), w_sib_send.at[b], sibling)
+
+    def w_wait(b):
+        w_push(other_w, b, w_sib_send.at[0], sibling).wait_recv()
+
+    def w_spread(b):
+        w_wait(core_block(b))
+
+        @pl.when(z % 3 == 0)
+        def _():
+            w_inward(b).start()
+
+        for way in range(2):
+            w_beside(b, way).start()
+        w_sib(b).start()
+
+    def w_hand_over(b):
+        w_wait(core_block(b))
+        w_sib(b).start()
+
+    @pl.when(z % 3 == 0)
+    def _():
+        for b in range(2):
+            w_edge(b).start()
+
+    for d in (4, 3, 5, 2, 6, 1, 7):
+        kv_copy(d).wait_send()
+    for d in (4, 3, 5, 2, 6, 1, 7):
+        q_copy(d).start()
     for d in range(1, SEQ):
         landed(kvr, kv_recv, (s + d) % SEQ)
     block = kvr[...].reshape(CT, 2 * HD)
@@ -175,55 +229,11 @@
             half_of(t, pair_of(n), right).wait_recv()
         sib_copy(n).start()
 
-    def block_of(place):
-        group = place // 4
-        step = group + group // 2 - 2 * (group // 3)
-        return 4 * ((x + step) % 4) + place % 4
-
-    def w_push(source, b, send, target):
-        return push(source.at[b], other_w.at[b], send, w_recv.at[b], target)
-
-    def core_block(b):
-        return block_of(4 * (b // 2) + 2 * k + b % 2)
-
-    def w_edge(b):
-        return w_push(own_w, core_block(b), w_edge_send.at[b], z_next(outward))
-
-    def w_inward(b):
-        return w_push(other_w, core_block(b), w_send.at[b, 0], z_next(-outward))
-
-    def w_beside(b, way):
-        target = (x_right, x_left, x_across)[way]
-        return w_push(other_w, core_block(b), w_send.at[b, 1 + way], target)
-
-    def w_sib(b):
-        return w_push(other_w, core_block(b), w_sib_send.at[b], sibling)
-
-    def w_wait(b):
-        w_push(other_w, b, w_sib_send.at[0], sibling).wait_recv()
-
-    def w_spread(b):
-        w_wait(core_block(b))
-
-        @pl.when(z % 3 == 0)
-        def _():
-            w_inward(b).start()
-
-        for way in range(3):
-            w_beside(b, way).start()
-        w_sib(b).start()
-
-    def w_hand_over(b):
-        w_wait(core_block(b))
-        w_sib(b).start()
-
     def pass_on(t):
         wait_slot(column_slot(t))
         spread(t)
 
     spread(0)
-    for d in (4, 3, 5, 2, 6, 1, 7):
-        q_copy(d).start()
     from_beside(0, 0)
     from_beside(0, 1)
 
@@ -244,10 +254,6 @@
     for b in range(BLOCKS):
         load_own(b).wait()
 
-    @pl.when(z % 3 == 0)
-    def _():
-        for b in range(2):
-            w_edge(b).start()
 
     load_mask.wait()
     load_level.wait()
@@ -311,8 +317,8 @@
             acc[:, cols] = acc[:, cols] * factor + update[:HD]
             ready = ahead
 
-    w_first = jnp.where(z == 2, 8, 3)
-    w_count = jnp.where(z == 1, 0, 2)
+    w_first = jnp.where(z == 0, 1, jnp.where(z == 1, 4, jnp.where(z == 2, 8, 1)))
+    w_count = 2
 
     def step(n, carry):
         t, i = (n // 4) // (1 + bottom), n % 4
@@ -375,11 +381,6 @@
     @pl.when(z == 3)
     def _():
         lse_swap.start()
-
-    @pl.when(w_count == 0)
-    def _():
-        w_spread(0)
-        w_spread(1)
 
     def gather_rows(source, first, place):
         for h in range(GROUP):
@@ -394,6 +395,10 @@
         mixed = part_of * home.astype(F32) + (1.0 - part_of) * far.astype(F32)
         return mixed.astype(BF16)
 
+    for group in (1, 2):
+        for half in range(2):
+            w_hand_over(2 * group + half)
+        w_across(2 - group).start()
     swap.wait()
 
     @pl.when(z == 3)
@@ -458,31 +463,27 @@
             done[:, cols] = (lat[:, cols].astype(F32) + gate_row * branch).astype(BF16)
             final(2 * j + dirn).start()
 
-    def tick(tau, carry):
-        @pl.when(tau >= 3 * LAG)
-        def _():
-            last(tau - 3 * LAG)
-
-        for hop in (2, 1):
-            @pl.when((tau >= hop * LAG) & (tau < NC + hop * LAG))
-            def _(hop=hop):
-                middle(hop, tau - hop * LAG)
-
-        @pl.when(tau < NC)
-        def _():
-            first(tau)
-
-        @pl.when((tau < 6) & (tau % 2 == 1))
-        def _():
-            w_hand_over(tau + 1)
-            w_hand_over(tau + 2)
-
-        return carry
-
-    lax.fori_loop(0, NC + 3 * LAG, tick, 0)
+    def run(lo, hi, work):
+        def body(j, carry):
+            work(j)
+            return carry
+
+        lax.fori_loop(lo, hi, body, 0)
+
+    early, late = NC // 2, NC
+    run(0, early, first)
+    run(0, early, lambda j: middle(1, j))
+    run(early, early + 2, first)
+    run(0, early, lambda j: middle(2, j))
+    w_hand_over(6)
+    w_hand_over(7)
+    run(early + 2, late, first)
+    run(early, late, lambda j: middle(1, j))
+    run(0, early, last)
+    run(early, late, lambda j: middle(2, j))
+    run(early, late, last)
 
     for d in range(1, SEQ):
-        kv_copy(d).wait_send()
         q_copy(d).wait_send()
 
     def drain_plane(t, carry):
@@ -518,8 +519,9 @@
             w_edge(b).wait_send()
             w_inward(b).wait_send()
 
-        for way in range(3):
+        for way in range(2):
             w_beside(b, way).wait_send()
+        w_across(b).wait_send()
     for b in range(8):
         w_sib(b).wait_send()
 

time: 110 us -> 94.3 us (0.86)
  the two profiles are of different devices: /device:TPU:64 before, /device:TPU:8 now
where the time goes in v6:
time: 94.3 us; the launch traced here: 94.2 us
  Pallas kernels  92.3 us (98%)
  local copies, waits for them, and re-layouts  1.92 us (2%)
    pallas_call x1, Pallas kernels, fused(): pl.pallas_call(kernel, out_shape=jax.ShapeDtypeStruct((ROWS, D), BF16), i...  92.3 us
    unnamed x1, local copies, waits for them, and re-layouts  1.92 us

profile of v6, /device:TPU:8, one launch (start us, length us, event | category | flops | bytes accessed | tf_op | source)
XLA Modules:
  0.0 94.2 jit_solution(10353977463204668815)
XLA Ops:
  0.0 92.3 %stretch_attention.1 = bf16[48,6144]{1,0:T(8,128)(2,1)} custom-call(bf16[48,24,128]{2,1,0:T(8,128)(2,1)} %q_raw.1, bf16[48,8,256]{2,1,0:T(8,128)(2,1)} %kv_raw.1, s32[32,32]{1,0:T(8,128)} %mask_hbm.1, s32[32]{0:T(128)} %level_hbm.1, bf16[384,6144]{1,0:T(8,128)(2,1)} %own_hbm.1, bf16[48,6144]{1,0:T(8,128)(2,1)} %lat_hbm.1, f32[64,6144]{1,0:T(8,128)} %gate_hbm.1), custom_call_target="tpu_custom_call" | custom-call | flops 5435817984 | bytes 20971520 | tf_op jit(solution)/shard_map/stretch_attention/pallas_call | solution.py:544
  92.3 1.9 %copy.9 = bf16[48,6144]{1,0:T(8,128)(2,1)} copy(bf16[48,6144]{1,0:T(8,128)(2,1)} %stretch_attention.1) | data formatting | bytes 1179648

commit v7 on v6

--- a/solution.py
+++ b/solution.py
@@ -296,10 +296,9 @@
                 jnp.dot(kb, q_cols, preferred_element_type=F32),
             )
 
-        ready = score(0)
+        scores = [score(r) for r in range(GROUP)]
         for r in range(GROUP):
-            ahead = score(r + 1) if r + 1 < GROUP else None
-            sa, sb = ready
+            sa, sb = scores[r]
             cols = slice(r * CT, (r + 1) * CT)
             top = jnp.maximum(
                 jnp.max(sa, axis=0, keepdims=True) - hide_a, jnp.max(sb, axis=0, keepdims=True) - hide_b
@@ -315,7 +314,6 @@
             )
             run_sum[:, cols] = run_sum[:, cols] * factor + update[HD : HD + 1]
             acc[:, cols] = acc[:, cols] * factor + update[:HD]
-            ready = ahead
 
     w_first = jnp.where(z == 0, 1, jnp.where(z == 1, 4, jnp.where(z == 2, 8, 1)))
     w_count = 2
@@ -359,9 +357,9 @@
 
         turn = n - w_first
 
-        @pl.when((turn >= 0) & (turn % 3 == 0) & (turn < 3 * w_count))
-        def _():
-            w_spread(turn // 3)
+        @pl.when((turn >= 0) & (turn % 2 == 0) & (turn < 2 * w_count))
+        def _():
+            w_spread(turn // 2)
 
         return carry
 
@@ -413,13 +411,11 @@
     gather_rows(att_in, 0, 1)
 
     def ring(hop, dirn, j):
+        target = y_up if (dirn == 0) == (hop < 2) else y_down
         return push(
             sends.at[hop, dirn, j], recvs.at[hop, dirn, j],
-            ring_send.at[hop, dirn, j], ring_recv.at[hop, dirn, j], y_down if dirn else y_up,
+            ring_send.at[hop, dirn, j], ring_recv.at[hop, dirn, j], target,
         )
-
-    def block_at(hop, dirn):
-        return (y + 1 + hop) % 4 if dirn else (y + 3 - hop) % 4
 
     def columns(place):
         return pl.ds(pl.multiple_of(block_of(place) * CT, CT), CT)
@@ -443,22 +439,26 @@
             product = jnp.dot(rows_in[0], own_w[q], preferred_element_type=F32)
             product += jnp.dot(rows_in[1], other_w[q], preferred_element_type=F32)
             part[dirn, j] = product.reshape(4, ROWS, CT)
-            sends[0, dirn, j] = part[dirn, j, block_at(0, dirn)].astype(BF16)
+            sends[0, dirn, j] = part[dirn, j, (y + 2) % 4].astype(BF16)
             ring(0, dirn, j).start()
-
-    def middle(hop, j):
         for dirn in range(2):
-            ring(hop - 1, dirn, j).wait_recv()
-            sends[hop, dirn, j] = (
-                recvs[hop - 1, dirn, j].astype(F32) + part[dirn, j, block_at(hop, dirn)]
+            sends[2, dirn, j] = part[dirn, j, (y + 3 - 2 * dirn) % 4].astype(BF16)
+            ring(2, dirn, j).start()
+
+    def middle(j):
+        for dirn in range(2):
+            ring(0, dirn, j).wait_recv()
+            sends[1, dirn, j] = (
+                recvs[0, dirn, j].astype(F32) + part[dirn, j, (y + 1 + 2 * dirn) % 4]
             ).astype(BF16)
-            ring(hop, dirn, j).start()
+            ring(1, dirn, j).start()
 
     def last(j):
         for dirn in range(2):
             cols = columns(2 * j + dirn)
+            ring(1, dirn, j).wait_recv()
             ring(2, dirn, j).wait_recv()
-            branch = recvs[2, dirn, j].astype(F32) + part[dirn, j, y]
+            branch = recvs[1, dirn, j].astype(F32) + recvs[2, dirn, j].astype(F32) + part[dirn, j, y]
             gate_row = gate[pl.ds(level, 1), cols]
             done[:, cols] = (lat[:, cols].astype(F32) + gate_row * branch).astype(BF16)
             final(2 * j + dirn).start()
@@ -470,18 +470,16 @@
 
         lax.fori_loop(lo, hi, body, 0)
 
-    early, late = NC // 2, NC
-    run(0, early, first)
-    run(0, early, lambda j: middle(1, j))
-    run(early, early + 2, first)
-    run(0, early, lambda j: middle(2, j))
+    run(0, 4, first)
+    run(0, 4, middle)
+    run(4, 6, first)
     w_hand_over(6)
     w_hand_over(7)
-    run(early + 2, late, first)
-    run(early, late, lambda j: middle(1, j))
-    run(0, early, last)
-    run(early, late, lambda j: middle(2, j))
-    run(early, late, last)
+    run(6, 8, first)
+    run(4, 6, middle)
+    run(0, 4, last)
+    run(6, 8, middle)
+    run(4, 8, last)
 
     for d in range(1, SEQ):
         q_copy(d).wait_send()

time: 94.3 us -> 91.8 us (0.973)
  Pallas kernels: 92.3 us -> 89.7 us
    pallas_call x1, Pallas kernels: 92.3 us -> 89.7 us  [fused(): pl.pallas_call(kernel, out_shape=jax.ShapeDtypeStruct((ROWS, D), BF16), i...]
where the time goes in v7:
time: 91.8 us; the launch traced here: 91.6 us
  Pallas kernels  89.7 us (98%)
  local copies, waits for them, and re-layouts  1.92 us (2%)
    pallas_call x1, Pallas kernels, fused(): pl.pallas_call(kernel, out_shape=jax.ShapeDtypeStruct((ROWS, D), BF16), i...  89.7 us
    unnamed x1, local copies, waits for them, and re-layouts  1.92 us

profile of v7, /device:TPU:8, one launch (start us, length us, event | category | flops | bytes accessed | tf_op | source)
XLA Modules:
  0.0 91.6 jit_solution(15141018404744075873)
XLA Ops:
  0.0 89.7 %stretch_attention.1 = bf16[48,6144]{1,0:T(8,128)(2,1)} custom-call(bf16[48,24,128]{2,1,0:T(8,128)(2,1)} %q_raw.1, bf16[48,8,256]{2,1,0:T(8,128)(2,1)} %kv_raw.1, s32[32,32]{1,0:T(8,128)} %mask_hbm.1, s32[32]{0:T(128)} %level_hbm.1, bf16[384,6144]{1,0:T(8,128)(2,1)} %own_hbm.1, bf16[48,6144]{1,0:T(8,128)(2,1)} %lat_hbm.1, f32[64,6144]{1,0:T(8,128)} %gate_hbm.1), custom_call_target="tpu_custom_call" | custom-call | flops 5435817984 | bytes 20971520 | tf_op jit(solution)/shard_map/stretch_attention/pallas_call | solution.py:542
  89.7 1.9 %copy.9 = bf16[48,6144]{1,0:T(8,128)(2,1)} copy(bf16[48,6144]{1,0:T(8,128)(2,1)} %stretch_attention.1) | data formatting | bytes 1179648

commit v8 on v7

--- a/solution.py
+++ b/solution.py
@@ -26,8 +26,8 @@
 
 
 def kernel(
-    q_raw, kv_raw, mask_hbm, level_hbm, own_hbm, lat_hbm, gate_hbm, out_ref,
-    q_ref, kv_ref, mask_ref, level_ref, q_far, att_far, mate_att, blend, lse, lse_partner, lse_mate, kvr, qr, qt, slots, acc, run_max, run_sum, att, att_in, rows_in,
+    q_hbm, kv_hbm, mask_hbm, level_hbm, own_hbm, lat_hbm, gate_hbm, out_ref,
+    q_raw, kv_raw, q_ref, kv_ref, mask_ref, level_ref, q_far, att_far, mate_att, blend, lse, lse_partner, lse_mate, kvr, qr, qt, slots, acc, run_max, run_sum, att, att_in, rows_in,
     own_w, other_w, part, sends, recvs, lat, gate, done,
     mate_send, mate_recv, kv_send, kv_recv, q_send, q_recv, z_send, down_send, x_send, relay_send, sib_send, slot_recv, half_recv,
     load_sem, w_edge_send, w_send, w_sib_send, w_recv, swap_sem, ring_send, ring_recv, out_send, out_recv,
@@ -74,13 +74,19 @@
     ]
     for target in greeted:
         pl.semaphore_signal(barrier, inc=1, device_id=target, device_id_type=MESH)
+    load_kv = pltpu.make_async_copy(kv_hbm, kv_raw, load_sem.at[BLOCKS + 4])
+    load_q = pltpu.make_async_copy(q_hbm, q_raw, load_sem.at[BLOCKS + 5])
+    load_kv.start()
+    load_q.start()
     load_mask.start()
     load_level.start()
     for b in range(BLOCKS):
         load_own(b).start()
     load_lat.start()
     load_gate.start()
+    load_kv.wait()
     kv_ref[...] = jnp.transpose(kv_raw[...], (1, 0, 2))
+    load_q.wait()
     q_ref[...] = jnp.transpose(q_raw[...], (1, 0, 2)).reshape(SEQ, GROUP, ROWS, HD)
     run_max[...] = jnp.full_like(run_max, -BIG)
     run_sum[...] = jnp.zeros_like(run_sum)
@@ -536,15 +542,16 @@
 
 
 def fused(queries, keys_values, mask, level, own, latents, gate_table):
-    vmem = pl.BlockSpec(memory_space=pltpu.VMEM)
     anywhere = pl.BlockSpec(memory_space=pl.ANY)
     dma = pltpu.SemaphoreType.DMA
     return pl.pallas_call(
         kernel,
         out_shape=jax.ShapeDtypeStruct((ROWS, D), BF16),
-        in_specs=[vmem, vmem] + [anywhere] * 5,
+        in_specs=[anywhere] * 7,
         out_specs=anywhere,
         scratch_shapes=[
+            pltpu.VMEM((ROWS, SEQ * GROUP, HD), BF16),
+            pltpu.VMEM((ROWS, SEQ, 2 * HD), BF16),
             pltpu.VMEM((SEQ, GROUP, ROWS, HD), BF16),
             pltpu.VMEM((SEQ, ROWS, 2 * HD), BF16),
             pltpu.SMEM((32, 32), jnp.int32),
@@ -576,7 +583,7 @@
             pltpu.VMEM((ROWS, D), BF16),
             dma((6,)), dma((6,)), dma((SEQ,)), dma((SEQ,)), dma((SEQ,)), dma((SEQ,)),
             dma((4,)), dma((1,)), dma((4, 2)), dma((4, 2)), dma((16,)), dma((32,)), dma((4, 2)),
-            dma((BLOCKS + 4,)), dma((2,)), dma((2, 4)), dma((8,)), dma((BLOCKS,)), dma((2,)),
+            dma((BLOCKS + 6,)), dma((2,)), dma((2, 4)), dma((8,)), dma((BLOCKS,)), dma((2,)),
             dma((3, 2, NC)), dma((3, 2, NC)), dma((BLOCKS,)), dma((BLOCKS,)),
         ],
         compiler_params=pltpu.CompilerParams(

time: 91.8 us -> 90.8 us (0.989)
  Pallas kernels: 89.7 us -> 88.7 us
    pallas_call x1, Pallas kernels: 89.7 us -> 88.7 us  [fused(): pl.pallas_call(kernel, out_shape=jax.ShapeDtypeStruct((ROWS, D), BF16), i...]
where the time goes in v8:
time: 90.8 us; the launch traced here: 90.6 us
  Pallas kernels  88.7 us (98%)
  local copies, waits for them, and re-layouts  1.92 us (2%)
    pallas_call x1, Pallas kernels, fused(): pl.pallas_call(kernel, out_shape=jax.ShapeDtypeStruct((ROWS, D), BF16), i...  88.7 us
    unnamed x1, local copies, waits for them, and re-layouts  1.92 us

profile of v8, /device:TPU:8, one launch (start us, length us, event | category | flops | bytes accessed | tf_op | source)
XLA Modules:
  0.0 90.6 jit_solution(8791718638445226784)
XLA Ops:
  0.0 88.7 %stretch_attention.1 = bf16[48,6144]{1,0:T(8,128)(2,1)} custom-call(bf16[48,24,128]{2,1,0:T(8,128)(2,1)} %q_hbm.1, bf16[48,8,256]{2,1,0:T(8,128)(2,1)} %kv_hbm.1, s32[32,32]{1,0:T(8,128)} %mask_hbm.1, s32[32]{0:T(128)} %level_hbm.1, bf16[384,6144]{1,0:T(8,128)(2,1)} %own_hbm.1, bf16[48,6144]{1,0:T(8,128)(2,1)} %lat_hbm.1, f32[64,6144]{1,0:T(8,128)} %gate_hbm.1), custom_call_target="tpu_custom_call" | custom-call | flops 5435817984 | bytes 20971520 | tf_op jit(solution)/shard_map/stretch_attention/pallas_call | solution.py:547
  88.7 1.9 %copy.9 = bf16[48,6144]{1,0:T(8,128)(2,1)} copy(bf16[48,6144]{1,0:T(8,128)(2,1)} %stretch_attention.1) | data formatting | bytes 1179648

commit v9 on v8

--- a/solution.py
+++ b/solution.py
@@ -321,7 +321,7 @@
             run_sum[:, cols] = run_sum[:, cols] * factor + update[HD : HD + 1]
             acc[:, cols] = acc[:, cols] * factor + update[:HD]
 
-    w_first = jnp.where(z == 0, 1, jnp.where(z == 1, 4, jnp.where(z == 2, 8, 1)))
+    w_first = jnp.where(z == 0, 1, jnp.where(z == 1, 5, jnp.where(z == 2, 8, 2)))
     w_count = 2
 
     def step(n, carry):
@@ -478,13 +478,11 @@
 
     run(0, 4, first)
     run(0, 4, middle)
-    run(4, 6, first)
     w_hand_over(6)
     w_hand_over(7)
-    run(6, 8, first)
-    run(4, 6, middle)
+    run(4, 8, first)
     run(0, 4, last)
-    run(6, 8, middle)
+    run(4, 8, middle)
     run(4, 8, last)
 
     for d in range(1, SEQ):

time: 90.8 us -> 88.7 us (0.977)
  Pallas kernels: 88.7 us -> 86.4 us
    pallas_call x1, Pallas kernels: 88.7 us -> 86.4 us  [fused(): pl.pallas_call(kernel, out_shape=jax.ShapeDtypeStruct((ROWS, D), BF16), i...]
where the time goes in v9:
time: 88.7 us; the launch traced here: 88.4 us
  Pallas kernels  86.4 us (97%)
  local copies, waits for them, and re-layouts  1.92 us (2%)
    pallas_call x1, Pallas kernels, fused(): pl.pallas_call(kernel, out_shape=jax.ShapeDtypeStruct((ROWS, D), BF16), i...  86.4 us
    unnamed x1, local copies, waits for them, and re-layouts  1.92 us

profile of v9, /device:TPU:8, one launch (start us, length us, event | category | flops | bytes accessed | tf_op | source)
XLA Modules:
  0.0 88.4 jit_solution(12499906021504788181)
XLA Ops:
  0.0 86.4 %stretch_attention.1 = bf16[48,6144]{1,0:T(8,128)(2,1)} custom-call(bf16[48,24,128]{2,1,0:T(8,128)(2,1)} %q_hbm.1, bf16[48,8,256]{2,1,0:T(8,128)(2,1)} %kv_hbm.1, s32[32,32]{1,0:T(8,128)} %mask_hbm.1, s32[32]{0:T(128)} %level_hbm.1, bf16[384,6144]{1,0:T(8,128)(2,1)} %own_hbm.1, bf16[48,6144]{1,0:T(8,128)(2,1)} %lat_hbm.1, f32[64,6144]{1,0:T(8,128)} %gate_hbm.1), custom_call_target="tpu_custom_call" | custom-call | flops 5435817984 | bytes 20971520 | tf_op jit(solution)/shard_map/stretch_attention/pallas_call | solution.py:545
  86.4 1.9 %copy.9 = bf16[48,6144]{1,0:T(8,128)(2,1)} copy(bf16[48,6144]{1,0:T(8,128)(2,1)} %stretch_attention.1) | data formatting | bytes 1179648
